TPU v7x, 128 devices: a whole 4x4x4 slice. The times are simulated.
128 devices in a mesh: pix: 8 (over x, core), mz: 16 (over z, y).
Axes of the slice: x: 4, y: 4, z: 4, core: 2. Of those that a mesh axis runs over, the one named last changes fastest.
Arguments:
- spectra: bfloat16 [256, 1024, 256], P('pix', 'mz'), may hold values from -40 to 40
- owner: int32 [384], replicated, may hold values from 0 to 15, as said below
- peaks: int32 [384, 4], replicated, may hold values from 0 to 255, as said below
- pattern_index: int32 [384], replicated, may hold values from 0 to 63
- patterns: float32 [64, 4], replicated, may hold values from 0.05 to 1
Outputs:
- ion_images: bfloat16 [256, 256, 1024], P('mz', 'pix')
- formula_images: bfloat16 [768, 256, 1024], P('mz', 'pix')
- chaos: float32 [768], P('mz')
Inputs may be any that keep to these rules, and one draw needn't show every extreme that they name: Each of the 16 owners has at most 48 formulas, and some owner has exactly 48. `peaks`: each formula's 4 bins rise strictly by equal steps of 1 to 4 bins.
All inputs are finite; a program needn't handle non-finite values.
Results may differ from a plain program's by a relative error of at most 0.0056.
Values may be sent and summed in bfloat16 or wider, within the bound.
A program may use at most 128 MiB of HBM per device.

v0:
```python
import math

import jax
import jax.numpy as jnp
from jax import lax
from jax.sharding import PartitionSpec as P

CAP = 48


gauss_raw = [math.exp(-offset * offset / 4.5) for offset in range(-3, 4)]
gauss_taps = [entry_value / sum(gauss_raw) for entry_value in gauss_raw]


def padded_2(block, sides, width):
    for axis, dim in sides:
        count = lax.axis_size(axis)
        forward = [(i, i + 1) for i in range(count - 1)]
        backward = [(target, source) for source, target in forward]
        low = lax.ppermute(
            lax.slice_in_dim(block, block.shape[dim] - width, None, axis=dim), axis, forward
        )
        high = lax.ppermute(lax.slice_in_dim(block, 0, width, axis=dim), axis, backward)
        block = jnp.concatenate([low, block, high], axis=dim)
    return block


def shifted(array, axis, by):
    size = lax.axis_size(axis)
    pairs = [(i, i + by) for i in range(size) if 0 <= i + by < size]
    return lax.ppermute(array, axis, pairs)


def blur_axis(padded, axis, count):
    total = gauss_taps[0] * lax.slice_in_dim(padded, 0, count, axis=axis)
    for offset in range(1, len(gauss_taps)):
        total = total + gauss_taps[offset] * lax.slice_in_dim(
            padded, offset, offset + count, axis=axis
        )
    return total


def slot_coefficients(owner, peaks, pattern_index, patterns, slots, bins, owners_count):
    owner_hot = (owner[:, None] == jnp.arange(owners_count)[None, :]).astype(jnp.int32)
    earlier = jnp.cumsum(owner_hot, axis=0) - owner_hot
    rank_in = jnp.sum(earlier * owner_hot, axis=1)
    slot_of = owner * (slots // owners_count) + rank_in
    pattern_hot = (pattern_index[:, None] == jnp.arange(patterns.shape[0])[None, :]).astype(
        jnp.float32
    )
    peak_weight = jnp.dot(pattern_hot, patterns, precision=lax.Precision.HIGHEST)
    peak_hot = (peaks[:, :, None] == jnp.arange(bins)[None, None, :]).astype(jnp.float32)
    per_formula = jnp.einsum("fk,fkb->fb", peak_weight, peak_hot, precision=lax.Precision.HIGHEST)
    slot_hot = (jnp.arange(slots)[:, None] == slot_of[None, :]).astype(jnp.float32)
    return jnp.dot(slot_hot, per_formula, precision=lax.Precision.HIGHEST).astype(jnp.bfloat16)


def body(spectra, owner, peaks, pattern_index, patterns):
    owners_count = lax.axis_size("mz")
    bins = spectra.shape[2]
    slots = owners_count * CAP
    rows_local = spectra.shape[0]
    strip_cols = spectra.shape[1]
    column_count = strip_cols * owners_count
    coef = slot_coefficients(owner, peaks, pattern_index, patterns, slots, bins, owners_count)
    images = lax.all_to_all(
        jnp.transpose(spectra, (2, 0, 1)), "mz", split_axis=0, concat_axis=2, tiled=True
    )
    padded = padded_2(images, (("pix", 1),), 3)
    rows_done = blur_axis(padded.astype(jnp.float32), 1, rows_local)
    rows_done = jnp.pad(rows_done, ((0, 0), (0, 0), (3, 3)))
    ion_images = blur_axis(rows_done, 2, column_count).astype(jnp.bfloat16)
    own_coef = lax.dynamic_slice_in_dim(coef, lax.axis_index("mz") * CAP, CAP, 0)
    empty = jnp.zeros((CAP, rows_local, column_count), jnp.float32)
    piece = lax.all_gather(ion_images, "mz", axis=0, tiled=True)
    flat = jnp.dot(
        own_coef,
        piece.reshape(piece.shape[0], rows_local * column_count),
        preferred_element_type=jnp.float32,
    )
    summed = flat.reshape(empty.shape)
    formula_images = summed.astype(jnp.bfloat16)
    values = formula_images.astype(jnp.float32)
    above = shifted(formula_images[:, -1, :], "pix", 1).astype(jnp.float32)
    has_above = (lax.axis_index("pix") > 0).astype(jnp.float32)
    across = values[:, :, 1:] - values[:, :, :-1]
    down = values[:, 1:, :] - values[:, :-1, :]
    seam_diff = values[:, 0, :] - above
    rough = jnp.sum(across * across, axis=(1, 2)) + jnp.sum(down * down, axis=(1, 2))
    rough = rough + has_above * jnp.sum(seam_diff * seam_diff, axis=1)
    energy = jnp.sum(values * values, axis=(1, 2))
    rough, energy = lax.psum((rough, energy), "pix")
    chaos = rough / (energy + 1e-05)
    return (ion_images, formula_images, chaos)


def solution(mesh):
    in_specs = (P("pix", "mz", None), P(), P(), P(), P())
    out_specs = (P("mz", "pix", None), P("mz", "pix", None), P("mz"))
    return jax.shard_map(body, mesh=mesh, in_specs=in_specs, out_specs=out_specs, check_vma=False)
```

profile of v0, /device:TPU:1, one launch (start us, length us, event | category | flops | bytes accessed | tf_op | source)
XLA Modules:
  0.0 242.5 jit_solution(11480819227906223242)
XLA Ops:
  7.2 3.9 %copy.23 = bf16[32,64,256]{1,0,2:T(8,128)(2,1)S(1)} copy(bf16[32,64,256]{2,1,0:T(8,128)(2,1)} %param.5) | data formatting | bytes 2097152 | tf_op args[0]
  11.1 1.5 reshape.36
  12.7 24.6 %all_to_all.18 = bf16[16,2,16384]{2,1,0:T(2,128)(2,1)} all-to-all(bf16[16,2,16384]{2,1,0:T(2,128)(2,1)S(1)} %reshape.36), channel_id=1, replica_groups=mesh['pix'=8,'mz'=16] {'mz'}, dimensions={0} | all-to-all | bytes 2097152 | tf_op jit(solution)/shard_map/all_to_all | solution.py:66
  37.3 3.8 %reshape.37 = bf16[256,32,64]{2,1,0:T(8,128)(2,1)S(1)} reshape(bf16[16,2,16384]{2,1,0:T(2,128)(2,1)} %all_to_all.18) | data formatting | bytes 2097152
  41.1 2.7 %copy.24 = bf16[16,32,16,64]{3,2,1,0:T(8,128)(2,1)} copy(bf16[16,32,16,64]{3,1,0,2:T(8,128)(2,1)S(1)} %bitcast.61) | data formatting | bytes 2097152 | tf_op jit(solution)/shard_map/all_to_all | solution.py:66
  43.7 3.2 %all_to_all.16 = bf16[16,32,1024]{2,1,0:T(8,128)(2,1)S(1)} reshape(bf16[16,32,16,64]{3,2,1,0:T(8,128)(2,1)} %copy.24) | data formatting | bytes 2097152 | tf_op jit(solution)/shard_map/all_to_all | solution.py:66
  47.1 3.9 %collective-permute-start.1 = (bf16[16,3,1024]{2,1,0:T(4,128)(2,1)S(1)}, bf16[16,3,1024]{2,1,0:T(4,128)(2,1)S(1)}, u32[]{:S(2)}, u32[]{:S(2)}) collective-permute-start(bf16[16,3,1024]{2,1,0:T(4,128)(2,1)S(1)} %get-tuple-element.18), channel_id=1, source_target_pairs={{16,0},{32,16},{48,32},{64,48},{80,64},{96,80},{112,96},{17,1},{33... | collective-permute-start | bytes 294920 | tf_op jit(solution)/shard_map/ppermute | solution.py:23
  51.0 3.2 %collective-permute-start = (bf16[16,3,1024]{2,1,0:T(4,128)(2,1)S(1)}, bf16[16,3,1024]{2,1,0:T(4,128)(2,1)S(1)}, u32[]{:S(2)}, u32[]{:S(2)}) collective-permute-start(bf16[16,3,1024]{2,1,0:T(4,128)(2,1)S(1)} %get-tuple-element.17), channel_id=1, source_target_pairs={{0,16},{16,32},{32,48},{48,64},{64,80},{80,96},{96,112},{1,17},{17... | collective-permute-start | bytes 294920 | tf_op jit(solution)/shard_map/ppermute | solution.py:20
  54.2 0.5 collective-permute-done.1
  54.7 1.2 collective-permute-done
  56.4 1.7 fusion.22
  58.2 4.2 %fusion.16 = bf16[16,32,1024]{2,1,0:T(8,128)(2,1)} fusion(f32[16,32,1024]{2,1,0:T(8,128)S(1)} %fusion.22), kind=kLoop, calls=%fused_computation.23 | loop fusion | flops 7340032 | bytes 3145728 | tf_op jit(solution)/shard_map/convert_element_type | solution.py:72
  62.5 0.9 reduce-window.6
  64.2 2.1 fusion.28
  66.2 0.8 fusion.29
  67.1 105.1 %all-gather.2.cloned.1.call-done = bf16[256,32,1024]{2,1,0:T(8,128)(2,1)} async-done(((bf16[16,32,1024]{2,1,0:T(8,128)(2,1)}), bf16[256,32,1024]{2,1,0:T(8,128)(2,1)}) %all-gather.2.cloned.1.call-update) | async-done | bytes 16777232 | tf_op jit(solution)/shard_map/all_gather | solution.py:75
  172.2 23.3 %copy.31 = bf16[256,32,1024]{0,2,1:T(8,128)(2,1)} copy(bf16[256,32,1024]{2,1,0:T(8,128)(2,1)} %all-gather.2.cloned.1.call-done) | data formatting | bytes 33554432 | tf_op jit(solution)/shard_map/reshape | solution.py:78
  195.5 13.4 %fusion.47 = (f32[48,32,1024]{2,0,1:T(8,128)}, bf16[48,32,1024]{2,0,1:T(8,128)(2,1)S(1)}) fusion(bf16[256,32,1024]{0,2,1:T(8,128)(2,1)} %copy.31, bf16[768,256]{1,0:T(8,128)(2,1)S(1)} %fusion.29, s32[]{:T(128)S(6)} %select_n.3), kind=kOutput, calls=%fused_computation.75 | convolution fusion | flops 808452096 | bytes 26238980 | tf_op jit(solution)/shard_map/dot_general | solution.py:76
  208.9 6.6 %fusion.3 = f32[48]{0:T(128)S(1)} fusion(f32[48,32,1024]{2,0,1:T(8,128)} %get-tuple-element.19), kind=kLoop, calls=%fused_computation.4 | loop fusion | flops 4713936 | bytes 12570816 | tf_op jit(solution)/shard_map/reduce_sum | solution.py:89
  215.5 0.8 fusion.5
  216.3 3.9 %collective-permute-start.2 = (bf16[48,1024]{1,0:T(8,128)(2,1)S(1)}, bf16[48,1024]{1,0:T(8,128)(2,1)S(1)}, u32[]{:S(2)}, u32[]{:S(2)}) collective-permute-start(bf16[48,1024]{1,0:T(8,128)(2,1)S(1)} %slice_bitcast_fusion.1), channel_id=1, source_target_pairs={{0,16},{16,32},{32,48},{48,64},{64,80},{80,96},{96,112},{1,17},{17... | collective-permute-start | bytes 294920 | tf_op jit(solution)/shard_map/ppermute | solution.py:31
  220.2 0.8 multiply_reduce_fusion
  221.0 3.4 %copy.28 = bf16[48,32,1024]{2,1,0:T(8,128)(2,1)} copy(bf16[48,32,1024]{2,0,1:T(8,128)(2,1)S(1)} %get-tuple-element.20) | data formatting | bytes 6291456
  224.5 10.6 %all-reduce.1 = (f32[48]{0:T(128)S(1)}, f32[48]{0:T(128)S(1)}) all-reduce(f32[48]{0:T(128)S(1)} %multiply_add_fusion.1, f32[48]{0:T(128)S(1)} %multiply_reduce_fusion), channel_id=1, replica_groups=mesh['pix'=8,'mz'=16] {'pix'}, use_global_device_ids=true, to_apply=%region_6.7 | all-reduce | flops 96 | bytes 768 | tf_op jit(solution)/shard_map/psum | solution.py:92
  (26 shorter events, 2.1 us)
Async XLA Ops:
  7.2 56.7 %copy-start = (f32[64,4]{0,1:T(4,128)S(1)}, f32[64,4]{0,1:T(4,128)}, u32[]{:S(2)}) copy-start(f32[64,4]{0,1:T(4,128)} %param.9) | copy-start | bytes 3076
  7.2 165.0 %all-gather.2.cloned.1.call-start = ((), (), s32[]{:S(2)}) async-start(), calls=%async_computation.1 | async-start | bytes 17825792 | tf_op jit(solution)/shard_map/all_gather | solution.py:75
  47.1 7.6 %collective-permute-start.1 = (bf16[16,3,1024]{2,1,0:T(4,128)(2,1)S(1)}, bf16[16,3,1024]{2,1,0:T(4,128)(2,1)S(1)}, u32[]{:S(2)}, u32[]{:S(2)}) collective-permute-start(bf16[16,3,1024]{2,1,0:T(4,128)(2,1)S(1)} %get-tuple-element.18), channel_id=1, source_target_pairs={{16,0},{32,16},{48,32},{64,48},{80,64},{96,80},{112,96},{17,1},{33... | collective-permute-start | bytes 294920 | tf_op jit(solution)/shard_map/ppermute | solution.py:23
  51.0 5.0 %collective-permute-start = (bf16[16,3,1024]{2,1,0:T(4,128)(2,1)S(1)}, bf16[16,3,1024]{2,1,0:T(4,128)(2,1)S(1)}, u32[]{:S(2)}, u32[]{:S(2)}) collective-permute-start(bf16[16,3,1024]{2,1,0:T(4,128)(2,1)S(1)} %get-tuple-element.17), channel_id=1, source_target_pairs={{0,16},{16,32},{32,48},{48,64},{64,80},{80,96},{96,112},{1,17},{17... | collective-permute-start | bytes 294920 | tf_op jit(solution)/shard_map/ppermute | solution.py:20
  58.1 4.3 %copy-start.2 = (s32[384]{0:T(512)S(1)}, s32[384]{0:T(512)}, u32[]{:S(2)}) copy-start(s32[384]{0:T(512)} %param.6) | copy-start | bytes 4612
  58.2 5.4 %copy-start.3 = (s32[384,4]{0,1:T(4,128)S(1)}, s32[384,4]{0,1:T(4,128)}, u32[]{:S(2)}) copy-start(s32[384,4]{0,1:T(4,128)} %param.7) | copy-start | bytes 18436
  58.2 5.7 %copy-start.4 = (s32[384]{0:T(512)S(1)}, s32[384]{0:T(512)}, u32[]{:S(2)}) copy-start(s32[384]{0:T(512)} %param.8) | copy-start | bytes 4612
  208.9 6.6 %copy-start.1 = (f32[48,32,1024]{2,0,1:T(8,128)S(1)}, f32[48,32,1024]{2,0,1:T(8,128)}, u32[]{:S(2)}) copy-start(f32[48,32,1024]{2,0,1:T(8,128)} %get-tuple-element.19) | copy-start | bytes 18874372
  216.3 8.1 %collective-permute-start.2 = (bf16[48,1024]{1,0:T(8,128)(2,1)S(1)}, bf16[48,1024]{1,0:T(8,128)(2,1)S(1)}, u32[]{:S(2)}, u32[]{:S(2)}) collective-permute-start(bf16[48,1024]{1,0:T(8,128)(2,1)S(1)} %slice_bitcast_fusion.1), channel_id=1, source_target_pairs={{0,16},{16,32},{32,48},{48,64},{64,80},{80,96},{96,112},{1,17},{17... | collective-permute-start | bytes 294920 | tf_op jit(solution)/shard_map/ppermute | solution.py:31
Sparse Core Ops, SparseCore 0:
  62.6 109.5 all-gather.1
where the time goes:
time: 244 us; the launch traced here: 242 us
  waiting for transfers between devices  107 us (44%)
  local copies, waits for them, and re-layouts  42.3 us (17%)
  blocking collectives  35.2 us (14%)
  matrix products  16.6 us (7%)
  other arithmetic  16.3 us (7%)
  between operations  14.2 us (6%)
  starting transfers between devices  11 us (5%)
    all_gather x1, waiting for transfers between devices, body(): piece = lax.all_gather(ion_images, 'mz', axis=0, tiled=True)  105 us
    all_to_all x1, blocking collectives, body(): lax.all_to_all(jnp.transpose(spectra, (2, 0, 1)), 'mz', split_axis=0, con...  24.6 us
    reshape x1, local copies, waits for them, and re-layouts, body(): piece.reshape(piece.shape[0], rows_local * column_count)  23.3 us
    dot_general x1, matrix products, body(): jnp.dot(own_coef, piece.reshape(piece.shape[0], rows_local * column_count...  13.4 us
    unnamed x15, local copies, waits for them, and re-layouts  12.8 us
    psum x1, blocking collectives, body(): rough, energy = lax.psum((rough, energy), 'pix')  10.6 us
    reduce_sum x1, other arithmetic, body(): jnp.sum(across * across, axis=(1, 2)) + jnp.sum(down * down, axis=(1, 2))  6.57 us
    all_to_all x2, local copies, waits for them, and re-layouts, body(): lax.all_to_all(jnp.transpose(spectra, (2, 0, 1)), 'mz', split_axis=0, con...  5.91 us
  transfers between devices with their start and end apart: 4, of which 3 were waited for; matrix products, arithmetic and copies ran while one was open for 4% of the time, Pallas kernels for 0%

commit v1 on v0

v1 whole, which is shorter than its diff:
```python
import math

import jax
import jax.numpy as jnp
import ml_dtypes
import numpy as np
from jax import lax
from jax.experimental import pallas as pl
from jax.experimental.pallas import tpu as pltpu
from jax.sharding import PartitionSpec as P

MESH = pl.DeviceIdType.MESH
F32, BF16 = jnp.float32, jnp.bfloat16

CAP = 48
N_MZ, N_PIX = 16, 8
SIDE = 4
ROWS, COLS, BINS = 32, 64, 256
GROUPS = ROWS // 4
PIXELS = ROWS * COLS
EXTRA = 128
TILES = (PIXELS + EXTRA) // 128
PARTS = 4

gauss_raw = [math.exp(-offset * offset / 4.5) for offset in range(-3, 4)]
taps = [value / sum(gauss_raw) for value in gauss_raw]

ORDER = [(0, 1), (1, 0), (0, 3), (3, 0), (1, 1), (3, 3), (1, 3), (3, 1), (2, 0), (0, 2), (2, 1), (1, 2), (2, 3), (3, 2), (2, 2)]


def tap(offset):
    return taps[offset + 3] if -3 <= offset <= 3 else 0.0


def split(matrix):
    high = matrix.astype(ml_dtypes.bfloat16)
    low = (matrix - high.astype(np.float64)).astype(ml_dtypes.bfloat16)
    return high, low


def constants():
    own = np.zeros((256, 256))
    sides = np.zeros((256, 32))
    pick = np.zeros((32, 256))
    for r in range(4):
        for c in range(COLS):
            for k in range(COLS):
                own[r * COLS + c, r * COLS + k] = tap(k - c)
            for j in range(4):
                sides[r * COLS + c, r * 4 + j] = tap(j - 4 - c)
                sides[r * COLS + c, 16 + r * 4 + j] = tap(COLS + j - c)
        for j in range(4):
            pick[r * 4 + j, r * COLS + j] = 1.0
            pick[16 + r * 4 + j, r * COLS + COLS - 4 + j] = 1.0
    seam = np.zeros((64, 320))
    for r in range(ROWS):
        for k in range(ROWS + 8):
            down = tap(k - 4 - r)
            for j in range(4):
                for edge in range(2):
                    seam[edge * 32 + r, k * 4 + j] = down * tap(j - 4 + 1 - edge)
                    seam[edge * 32 + r, 160 + k * 4 + j] = down * tap(j + 1 - edge)
    own_high, own_low = split(own)
    sides_high, sides_low = split(sides)
    blank = np.zeros((256, 64), ml_dtypes.bfloat16)
    first = np.concatenate([own_high, own_low, sides_high, sides_low, blank], axis=1)
    seam_high, seam_low = split(seam)
    second = np.zeros((96, 640), ml_dtypes.bfloat16)
    second[:64] = np.concatenate([seam_high, seam_low], axis=1)
    second[64:, :256] = pick.astype(ml_dtypes.bfloat16)
    return first, second


def dot(a, b):
    return jnp.dot(a, b, preferred_element_type=F32)


def dot_nt(a, b):
    return lax.dot_general(a, b, (((1,), (1,)), ((), ())), preferred_element_type=F32)


def iota(shape, axis):
    return lax.broadcasted_iota(jnp.int32, shape, axis)


def produce_kernel(
    spectra, owner, peaks, pattern_index, patterns, blur, more, parts, score,
    xs, pack_left, pack_right, left, right, ys, ion, coef, form, out, note, notes, total, totals,
    load_sem, halo_send, halo_recv, part_send, part_recv, part_own, note_send, note_recv, total_send, total_recv,
):
    pix, mz = lax.axis_index("pix"), lax.axis_index("mz")
    z, y = mz // SIDE, mz % SIDE

    def device(dp, dm):
        return {"pix": (pix + dp + N_PIX) % N_PIX, "mz": (mz + dm + N_MZ) % N_MZ}

    def peer(dz, dy):
        return ((z + dz) % SIDE) * SIDE + (y + dy) % SIDE

    def remote(src, dst, send, recv, target):
        return pltpu.make_async_remote_copy(
            src_ref=src, dst_ref=dst, send_sem=send, recv_sem=recv, device_id=target, device_id_type=MESH
        )

    load = pltpu.make_async_copy(spectra, xs.at[pl.ds(1, GROUPS)], load_sem)
    load.start()

    barrier = pltpu.get_barrier_semaphore()
    near = [(0, 1), (0, -1), (1, 0), (-1, 0), (1, 1), (1, -1), (-1, 1), (-1, -1)]
    for dp, dm in near[2:]:
        pl.semaphore_signal(barrier, inc=1, device_id=device(dp, dm), device_id_type=MESH)
    for dz, dy in ORDER:
        pl.semaphore_signal(barrier, inc=1, device_id={"mz": peer(dz, dy)}, device_id_type=MESH)
    for dp in range(2, N_PIX - 1):
        pl.semaphore_signal(barrier, inc=1, device_id=device(dp, 0), device_id_type=MESH)

    load.wait()
    pick = more[64:96, 0:256]

    def pack(g, carry):
        ends = dot(pick, xs[g]).astype(BF16)
        pack_left[g] = ends[0:16]
        pack_right[g] = ends[16:32]
        return carry

    lax.fori_loop(1, GROUPS + 1, pack, 0)
    pl.semaphore_wait(barrier, 6 + len(ORDER) + N_PIX - 3)

    inner = pl.ds(1, GROUPS)
    halo = [
        (xs.at[GROUPS], xs.at[0], (1, 0)),
        (xs.at[1], xs.at[GROUPS + 1], (-1, 0)),
        (pack_right.at[inner], left.at[inner], (0, 1)),
        (pack_left.at[inner], right.at[inner], (0, -1)),
        (pack_right.at[GROUPS], left.at[0], (1, 1)),
        (pack_right.at[1], left.at[GROUPS + 1], (-1, 1)),
        (pack_left.at[GROUPS], right.at[0], (1, -1)),
        (pack_left.at[1], right.at[GROUPS + 1], (-1, -1)),
    ]
    halo = [
        remote(src, dst, halo_send.at[i], halo_recv.at[i], device(*to)) for i, (src, dst, to) in enumerate(halo)
    ]
    for copy in halo:
        copy.start()

    blur_high, blur_low, blur_sides = blur[:, 0:256], blur[:, 256:512], blur[:, 512:576]

    def columns_own(g, carry):
        x = xs[g]
        ys[g] = dot(blur_high, x) + dot(blur_low, x)
        return carry

    lax.fori_loop(1, GROUPS + 1, columns_own, 0)

    count = owner.shape[1]
    owner_hot = (iota((N_MZ, count), 0) == owner[...]).astype(F32)
    before = (iota((count, count), 0) < iota((count, count), 1)).astype(F32).astype(BF16)
    earlier = dot(owner_hot.astype(BF16), before)
    rank = jnp.sum(earlier * owner_hot, axis=0, keepdims=True)
    slot = owner[...] * CAP + rank.astype(jnp.int32)
    pattern_hot = (iota((patterns.shape[1], count), 0) == pattern_index[...]).astype(F32).astype(BF16)
    weight = dot(patterns[...].astype(BF16), pattern_hot)
    spread = jnp.zeros((BINS, count), F32)
    for k in range(peaks.shape[0]):
        spread += jnp.where(iota((BINS, count), 0) == peaks[k : k + 1, :], weight[k : k + 1, :], 0.0)
    spread = spread.astype(BF16)
    place = iota((256, count), 0)
    place = (place // 16) * CAP + place % 16
    coef[0] = (iota((256, BINS), 0) == iota((256, BINS), 1)).astype(F32).astype(BF16)
    for q in range(1, PARTS):
        slot_hot = (place + (q - 1) * 16 == slot).astype(F32).astype(BF16)
        coef[q] = dot_nt(slot_hot, spread).astype(BF16)

    for copy in halo:
        copy.wait()

    @pl.when(pix == 0)
    def _():
        xs[0] = jnp.zeros(xs.shape[1:], BF16)
        left[0] = jnp.zeros(left.shape[1:], BF16)
        right[0] = jnp.zeros(right.shape[1:], BF16)

    @pl.when(pix == N_PIX - 1)
    def _():
        xs[GROUPS + 1] = jnp.zeros(xs.shape[1:], BF16)
        left[GROUPS + 1] = jnp.zeros(left.shape[1:], BF16)
        right[GROUPS + 1] = jnp.zeros(right.shape[1:], BF16)

    @pl.when(mz == 0)
    def _():
        left[...] = jnp.zeros(left.shape, BF16)

    @pl.when(mz == N_MZ - 1)
    def _():
        right[...] = jnp.zeros(right.shape, BF16)

    columns_own(0, 0)
    columns_own(GROUPS + 1, 0)

    def columns_sides(g, carry):
        sides = jnp.concatenate([left[g], right[g], left[g], right[g]], axis=0)
        ys[g] += dot(blur_sides, sides)
        return carry

    lax.fori_loop(0, GROUPS + 2, columns_sides, 0)

    for g in (0, GROUPS + 1):
        pack_left[g] = dot(pick[0:16], xs[g]).astype(BF16)
    edge = jnp.concatenate([left[...].reshape(160, BINS), pack_left[...].reshape(160, BINS)], axis=0)
    ion[PIXELS + 64 : PIXELS + 128] = (dot(more[0:64, 0:320], edge) + dot(more[0:64, 320:640], edge)).astype(BF16)

    def row(k, first):
        result = taps[3] * first(k + 3)
        for i in range(3):
            result = result + taps[i] * (first(k + i) + first(k + 6 - i))
        return result

    def slab(k):
        return ys[k // 4, pl.ds(pl.multiple_of((k % 4) * COLS, COLS), COLS), :]

    def rows(r, carry):
        at = pl.multiple_of((r % 16) * 128 + (r // 16) * 64, 64)
        ion[pl.ds(at, COLS), :] = row(r + 1, slab).astype(BF16)
        return carry

    lax.fori_loop(0, ROWS, rows, 0)
    ion[PIXELS : PIXELS + 64] = row(0, slab).astype(BF16)

    def product(q):
        def tile(n, carry):
            at = pl.multiple_of(n * 256, 256)
            result = dot_nt(coef[q], ion[pl.ds(at, 256), :])
            form[q, pl.ds(pl.multiple_of(n * 512, 512), 256), :] = result[:, 0:128]
            form[q, pl.ds(pl.multiple_of(n * 512 + 256, 256), 256), :] = result[:, 128:256]
            return carry

        lax.fori_loop(0, PIXELS // 256, tile, 0)
        form[q, pl.ds(PIXELS * 2, 256), :] = dot_nt(coef[q], ion[pl.ds(PIXELS, 128), :])

        def turn(d, carry):
            for s in range(16):
                out[q, d, s] = form[q, pl.ds(d * 16 + s, 16, stride=256), :].astype(BF16)
            return carry

        lax.fori_loop(0, N_MZ, turn, 0)

    def send(q):
        copies = []
        for i, (dz, dy) in enumerate(ORDER):
            to = peer(dz, dy)
            copies.append(
                remote(out.at[q, to], parts.at[q, mz], part_send.at[q, i], part_recv.at[q, i], {"mz": to})
            )
        copies.append(pltpu.make_async_copy(out.at[q, mz], parts.at[q, mz], part_own.at[q]))
        for copy in copies:
            copy.start()
        return copies

    product(0)
    copies = send(0)
    product(1)
    copies += send(1)
    product(2)
    product(3)

    lane, sub = iota((8, 128), 1), iota((8, 128), 0)
    keep_across = (lane % 64 != 0).astype(F32)
    keep_seam = jnp.where(mz > 0, (lane >= 96).astype(F32), 0.0)
    keep_top = jnp.where(pix > 0, 1.0, jnp.where(lane < 64, 0.0, 1.0))
    note[...] = jnp.zeros(note.shape, F32)

    for q in range(1, PARTS):
        def scores(d, carry, q=q):
            acc = jnp.zeros((8, 128), F32)
            for half in range(2):
                def value(j):
                    at = pl.multiple_of(j * 256 + d * 16 + half * 8, 8)
                    return form[q, pl.ds(at, 8), :].astype(BF16).astype(F32)

                extra = value(TILES - 1)
                prior = jnp.where(lane < 64, extra, pltpu.roll(value(15), 64, 1))
                across = jnp.zeros((8, 128), F32)
                down = jnp.zeros((8, 128), F32)
                energy = jnp.zeros((8, 128), F32)
                for j in range(16):
                    now = value(j)
                    step = now - pltpu.roll(now, 1, 1)
                    across += step * step
                    step = now - prior
                    if j == 0:
                        step = step * keep_top
                    down += step * step
                    energy += now * now
                    prior = now
                step = extra - pltpu.roll(extra, 32, 1)
                rough = across * keep_across + down + step * step * keep_seam
                rough = jnp.sum(rough, axis=1, keepdims=True)
                energy = jnp.sum(energy, axis=1, keepdims=True)
                base = (q - 1) * 16 + half * 8
                acc += jnp.where(lane == sub + base, rough, 0.0) + jnp.where(lane == sub + base + 64, energy, 0.0)
            note[d] += acc
            return carry

        lax.fori_loop(0, N_MZ, scores, 0)

    small = []
    for i, (dz, dy) in enumerate(ORDER):
        to = peer(dz, dy)
        small.append(remote(note.at[to], notes.at[mz], note_send.at[i], note_recv.at[i], {"mz": to}))
    for copy in small:
        copy.start()
    copies += send(2)
    for copy in small:
        copy.wait()
    notes[mz] = note[mz]
    total[...] = jnp.sum(notes[...], axis=0)
    small = []
    for dp in range(1, N_PIX):
        to = device(dp, 0)
        small.append(remote(total, totals.at[pix], total_send.at[dp], total_recv.at[dp], to))
    for copy in small:
        copy.start()
    copies += send(3)
    for copy in small:
        copy.wait()
    totals[pix] = total[...]
    final = jnp.sum(jnp.sum(totals[...], axis=0), axis=0, keepdims=True)
    final = final / (pltpu.roll(final, 64, 1) + 1e-5)
    score[...] = jnp.broadcast_to(final, (8, 128))
    for copy in copies:
        copy.wait()


def place_kernel(parts, score, ion_out, form_out, chaos_out):
    step = pl.program_id(0)

    def fill(target):
        def one(s, carry):
            for j in range(N_MZ // 2):
                a, b = parts[0, 2 * j, s], parts[0, 2 * j + 1, s]
                at = slice(j * 128, (j + 1) * 128)
                target[s, 0:16, at] = jnp.concatenate([a[:, :64], b[:, :64]], axis=1)
                target[s, 16:32, at] = jnp.concatenate([a[:, 64:], b[:, 64:]], axis=1)
            return carry

        lax.fori_loop(0, 16, one, 0)

    @pl.when(step == 0)
    def _():
        fill(ion_out)
        chaos_out[...] = score[...]

    @pl.when(step > 0)
    def _():
        fill(form_out)


def body(spectra, owner, peaks, pattern_index, patterns):
    first, second = constants()
    vmem = pl.BlockSpec(memory_space=pltpu.VMEM)
    hbm = pl.BlockSpec(memory_space=pl.ANY)
    dma = pltpu.SemaphoreType.DMA
    peers = len(ORDER)
    parts, score = pl.pallas_call(
        produce_kernel,
        out_shape=(
            jax.ShapeDtypeStruct((PARTS, N_MZ, 16, 16, 128), BF16),
            jax.ShapeDtypeStruct((8, 128), F32),
        ),
        in_specs=[hbm] + [vmem] * 6,
        out_specs=(hbm, vmem),
        scratch_shapes=[
            pltpu.VMEM((GROUPS + 2, 256, BINS), BF16),
            pltpu.VMEM((GROUPS + 2, 16, BINS), BF16),
            pltpu.VMEM((GROUPS + 2, 16, BINS), BF16),
            pltpu.VMEM((GROUPS + 2, 16, BINS), BF16),
            pltpu.VMEM((GROUPS + 2, 16, BINS), BF16),
            pltpu.VMEM((GROUPS + 2, 256, BINS), F32),
            pltpu.VMEM((PIXELS + EXTRA, BINS), BF16),
            pltpu.VMEM((PARTS, 256, BINS), BF16),
            pltpu.VMEM((PARTS, TILES * 256, 128), F32),
            pltpu.VMEM((PARTS, N_MZ, 16, 16, 128), BF16),
            pltpu.VMEM((N_MZ, 8, 128), F32),
            pltpu.VMEM((N_MZ, 8, 128), F32),
            pltpu.VMEM((8, 128), F32),
            pltpu.VMEM((N_PIX, 8, 128), F32),
            dma,
            dma((8,)),
            dma((8,)),
            dma((PARTS, peers)),
            dma((PARTS, peers)),
            dma((PARTS,)),
            dma((peers,)),
            dma((peers,)),
            dma((N_PIX,)),
            dma((N_PIX,)),
        ],
        compiler_params=pltpu.CompilerParams(
            collective_id=0, has_side_effects=True, vmem_limit_bytes=48 * 2**20
        ),
    )(
        spectra.reshape(GROUPS, 256, BINS),
        owner.reshape(1, -1),
        peaks.T,
        pattern_index.reshape(1, -1),
        patterns.T,
        jnp.asarray(first),
        jnp.asarray(second),
    )
    ion_images, formula_images, chaos = pl.pallas_call(
        place_kernel,
        grid=(PARTS,),
        out_shape=(
            jax.ShapeDtypeStruct((16, ROWS, COLS * N_MZ), BF16),
            jax.ShapeDtypeStruct((CAP, ROWS, COLS * N_MZ), BF16),
            jax.ShapeDtypeStruct((8, 128), F32),
        ),
        in_specs=[
            pl.BlockSpec((1, N_MZ, 16, 16, 128), lambda i: (i, 0, 0, 0, 0)),
            pl.BlockSpec((8, 128), lambda i: (0, 0)),
        ],
        out_specs=(
            pl.BlockSpec((16, ROWS, COLS * N_MZ), lambda i: (0, 0, 0)),
            pl.BlockSpec((16, ROWS, COLS * N_MZ), lambda i: (jnp.maximum(i, 1) - 1, 0, 0)),
            pl.BlockSpec((8, 128), lambda i: (0, 0)),
        ),
        compiler_params=pltpu.CompilerParams(vmem_limit_bytes=32 * 2**20),
    )(parts, score)
    return ion_images, formula_images, chaos[0, :CAP]


def solution(mesh):
    in_specs = (P("pix", "mz", None), P(), P(), P(), P())
    out_specs = (P("mz", "pix", None), P("mz", "pix", None), P("mz"))
    return jax.shard_map(body, mesh=mesh, in_specs=in_specs, out_specs=out_specs, check_vma=False)
```

time: 244 us -> 88.9 us (0.36)
  the two profiles are of different devices: /device:TPU:1 before, /device:TPU:11 now
where the time goes in v1:
time: 88.9 us; the launch traced here: 88.6 us
  Pallas kernels  81.6 us (92%)
  local copies, waits for them, and re-layouts  6.35 us (7%)
    pallas_call x1, Pallas kernels, body(): pl.pallas_call(produce_kernel, out_shape=(jax.ShapeDtypeStruct((PARTS, N_...  74.7 us
    pallas_call x1, Pallas kernels, body(): pl.pallas_call(place_kernel, grid=(PARTS,), out_shape=(jax.ShapeDtypeStru...  6.92 us
    unnamed x10, local copies, waits for them, and re-layouts  4.47 us

profile of v1, /device:TPU:11, one launch (start us, length us, event | category | flops | bytes accessed | tf_op | source)
XLA Modules:
  0.0 88.6 jit_solution(11990251658047946028)
XLA Ops:
  0.6 0.7 reshape.16.owner
  1.3 0.7 reshape.17.pattern_index
  2.0 0.0 copy-start
  2.0 1.2 %copy-done = bf16[32,64,256]{2,1,0:T(8,128)(2,1)S(1)} copy-done((bf16[32,64,256]{2,1,0:T(8,128)(2,1)S(1)}, bf16[32,64,256]{2,1,0:T(8,128)(2,1)}, u32[]{:S(2)}) %copy-start) | copy-done | bytes 1048600
  3.2 0.0 copy-start.1
  3.2 1.0 %copy-done.1 = bf16[256,640]{1,0:T(8,128)(2,1)S(1)} copy-done((bf16[256,640]{1,0:T(8,128)(2,1)S(1)}, bf16[256,640]{1,0:T(8,128)(2,1)}, u32[]{:S(2)}) %copy-start.1) | copy-done | bytes 327704
  4.2 0.0 copy-start.2
  4.2 0.9 %copy-done.2 = bf16[96,640]{1,0:T(8,128)(2,1)S(1)} copy-done((bf16[96,640]{1,0:T(8,128)(2,1)S(1)}, bf16[96,640]{1,0:T(8,128)(2,1)}, u32[]{:S(2)}) %copy-start.2) | copy-done | bytes 122904
  5.1 0.0 copy-start.3
  5.1 0.7 copy-done.3
  5.8 0.0 copy-start.4
  5.8 0.7 copy-done.4
  6.5 74.7 %shard_map.94 = (bf16[4,16,16,16,128]{4,3,2,1,0:T(8,128)(2,1)S(1)}, f32[8,128]{1,0:T(8,128)S(1)}) custom-call(bf16[8,256,256]{2,1,0:T(8,128)(2,1)S(1)} %bitcast.5, s32[1,384]{1,0:T(1,128)S(1)} %reshape.16.owner, s32[4,384]{1,0:T(4,128)S(1)} %bitcast.6, s32[1,384]{1,0:T(1,128)S(1)} %reshape.17.pattern_index, f32[4,64]{1,0:T(4,128)S(1)} %bitcast.7, ...), custom_call_target="tpu_custom_call" | custom-call | tf_op jit(solution)/shard_map/pallas_call | solution.py:364
  81.2 6.9 %shard_map.95 = (bf16[16,32,1024]{2,1,0:T(8,128)(2,1)}, bf16[48,32,1024]{2,1,0:T(8,128)(2,1)}, f32[8,128]{1,0:T(8,128)S(1)}) custom-call(bf16[4,16,16,16,128]{4,3,2,1,0:T(8,128)(2,1)S(1)} %get-tuple-element.8.parts, f32[8,128]{1,0:T(8,128)S(1)} %get-tuple-element.9.score), custom_call_target="tpu_custom_call" | custom-call | tf_op jit(solution)/shard_map/pallas_call | solution.py:410
  88.1 0.5 slice_bitcast_fusion
Async XLA Ops:
  2.0 1.2 %copy-start = (bf16[32,64,256]{2,1,0:T(8,128)(2,1)S(1)}, bf16[32,64,256]{2,1,0:T(8,128)(2,1)}, u32[]{:S(2)}) copy-start(bf16[32,64,256]{2,1,0:T(8,128)(2,1)} %param.7) | copy-start | bytes 3145732
  3.2 1.0 %copy-start.1 = (bf16[256,640]{1,0:T(8,128)(2,1)S(1)}, bf16[256,640]{1,0:T(8,128)(2,1)}, u32[]{:S(2)}) copy-start(bf16[256,640]{1,0:T(8,128)(2,1)} %constant.4.clone.blur) | copy-start | bytes 983044
  4.2 0.9 %copy-start.2 = (bf16[96,640]{1,0:T(8,128)(2,1)S(1)}, bf16[96,640]{1,0:T(8,128)(2,1)}, u32[]{:S(2)}) copy-start(bf16[96,640]{1,0:T(8,128)(2,1)} %constant.5.clone.more) | copy-start | bytes 368644
  5.1 0.7 copy-start.3
  5.8 0.7 copy-start.4

commit v2 on v1

--- a/solution.py
+++ b/solution.py
@@ -84,8 +84,8 @@
 
 
 def produce_kernel(
-    spectra, owner, peaks, pattern_index, patterns, blur, more, parts, score,
-    xs, pack_left, pack_right, left, right, ys, ion, coef, form, out, note, notes, total, totals,
+    spectra, owner_in, peaks_in, pattern_index_in, patterns_in, blur_in, more_in, parts, score,
+    owner, peaks, pattern_index, patterns, blur, more, xs, pack_left, pack_right, left, right, ys, ion, coef, form, out, note, notes, total, totals,
     load_sem, halo_send, halo_recv, part_send, part_recv, part_own, note_send, note_recv, total_send, total_recv,
 ):
     pix, mz = lax.axis_index("pix"), lax.axis_index("mz")
@@ -102,8 +102,11 @@
             src_ref=src, dst_ref=dst, send_sem=send, recv_sem=recv, device_id=target, device_id_type=MESH
         )
 
-    load = pltpu.make_async_copy(spectra, xs.at[pl.ds(1, GROUPS)], load_sem)
-    load.start()
+    sources = [spectra, more_in, blur_in, owner_in, peaks_in, pattern_index_in, patterns_in]
+    targets = [xs.at[pl.ds(1, GROUPS)], more, blur, owner, peaks, pattern_index, patterns]
+    loads = [pltpu.make_async_copy(src, dst, load_sem.at[i]) for i, (src, dst) in enumerate(zip(sources, targets))]
+    for copy in loads:
+        copy.start()
 
     barrier = pltpu.get_barrier_semaphore()
     near = [(0, 1), (0, -1), (1, 0), (-1, 0), (1, 1), (1, -1), (-1, 1), (-1, -1)]
@@ -114,7 +117,8 @@
     for dp in range(2, N_PIX - 1):
         pl.semaphore_signal(barrier, inc=1, device_id=device(dp, 0), device_id_type=MESH)
 
-    load.wait()
+    for copy in loads:
+        copy.wait()
     pick = more[64:96, 0:256]
 
     def pack(g, carry):
@@ -152,13 +156,14 @@
 
     lax.fori_loop(1, GROUPS + 1, columns_own, 0)
 
-    count = owner.shape[1]
-    owner_hot = (iota((N_MZ, count), 0) == owner[...]).astype(F32)
+    count = owner.shape[0]
+    owner_row = owner[...].reshape(1, count)
+    owner_hot = (iota((N_MZ, count), 0) == owner_row).astype(F32)
     before = (iota((count, count), 0) < iota((count, count), 1)).astype(F32).astype(BF16)
     earlier = dot(owner_hot.astype(BF16), before)
     rank = jnp.sum(earlier * owner_hot, axis=0, keepdims=True)
-    slot = owner[...] * CAP + rank.astype(jnp.int32)
-    pattern_hot = (iota((patterns.shape[1], count), 0) == pattern_index[...]).astype(F32).astype(BF16)
+    slot = owner_row * CAP + rank.astype(jnp.int32)
+    pattern_hot = (iota((patterns.shape[1], count), 0) == pattern_index[...].reshape(1, count)).astype(F32).astype(BF16)
     weight = dot(patterns[...].astype(BF16), pattern_hot)
     spread = jnp.zeros((BINS, count), F32)
     for k in range(peaks.shape[0]):
@@ -335,15 +340,11 @@
     step = pl.program_id(0)
 
     def fill(target):
-        def one(s, carry):
-            for j in range(N_MZ // 2):
-                a, b = parts[0, 2 * j, s], parts[0, 2 * j + 1, s]
-                at = slice(j * 128, (j + 1) * 128)
-                target[s, 0:16, at] = jnp.concatenate([a[:, :64], b[:, :64]], axis=1)
-                target[s, 16:32, at] = jnp.concatenate([a[:, 64:], b[:, 64:]], axis=1)
-            return carry
-
-        lax.fori_loop(0, 16, one, 0)
+        for j in range(N_MZ // 2):
+            a, b = parts[step, 2 * j], parts[step, 2 * j + 1]
+            at = slice(j * 128, (j + 1) * 128)
+            target[:, 0:16, at] = jnp.concatenate([a[:, :, :64], b[:, :, :64]], axis=2)
+            target[:, 16:32, at] = jnp.concatenate([a[:, :, 64:], b[:, :, 64:]], axis=2)
 
     @pl.when(step == 0)
     def _():
@@ -357,8 +358,6 @@
 
 def body(spectra, owner, peaks, pattern_index, patterns):
     first, second = constants()
-    vmem = pl.BlockSpec(memory_space=pltpu.VMEM)
-    hbm = pl.BlockSpec(memory_space=pl.ANY)
     dma = pltpu.SemaphoreType.DMA
     peers = len(ORDER)
     parts, score = pl.pallas_call(
@@ -367,9 +366,15 @@
             jax.ShapeDtypeStruct((PARTS, N_MZ, 16, 16, 128), BF16),
             jax.ShapeDtypeStruct((8, 128), F32),
         ),
-        in_specs=[hbm] + [vmem] * 6,
-        out_specs=(hbm, vmem),
+        in_specs=[pl.BlockSpec(memory_space=pltpu.HBM)] * 7,
+        out_specs=(pl.BlockSpec(memory_space=pl.ANY), pl.BlockSpec(memory_space=pltpu.VMEM)),
         scratch_shapes=[
+            pltpu.VMEM(owner.shape, jnp.int32),
+            pltpu.VMEM(peaks.shape[::-1], jnp.int32),
+            pltpu.VMEM(pattern_index.shape, jnp.int32),
+            pltpu.VMEM(patterns.shape[::-1], F32),
+            pltpu.VMEM(first.shape, BF16),
+            pltpu.VMEM(second.shape, BF16),
             pltpu.VMEM((GROUPS + 2, 256, BINS), BF16),
             pltpu.VMEM((GROUPS + 2, 16, BINS), BF16),
             pltpu.VMEM((GROUPS + 2, 16, BINS), BF16),
@@ -384,7 +389,7 @@
             pltpu.VMEM((N_MZ, 8, 128), F32),
             pltpu.VMEM((8, 128), F32),
             pltpu.VMEM((N_PIX, 8, 128), F32),
-            dma,
+            dma((7,)),
             dma((8,)),
             dma((8,)),
             dma((PARTS, peers)),
@@ -399,13 +404,13 @@
             collective_id=0, has_side_effects=True, vmem_limit_bytes=48 * 2**20
         ),
     )(
-        spectra.reshape(GROUPS, 256, BINS),
-        owner.reshape(1, -1),
+        *[pltpu.with_memory_space_constraint(x, pltpu.HBM) for x in (spectra.reshape(GROUPS, 256, BINS),
+        owner,
         peaks.T,
-        pattern_index.reshape(1, -1),
+        pattern_index,
         patterns.T,
         jnp.asarray(first),
-        jnp.asarray(second),
+        jnp.asarray(second))]
     )
     ion_images, formula_images, chaos = pl.pallas_call(
         place_kernel,
@@ -416,8 +421,8 @@
             jax.ShapeDtypeStruct((8, 128), F32),
         ),
         in_specs=[
-            pl.BlockSpec((1, N_MZ, 16, 16, 128), lambda i: (i, 0, 0, 0, 0)),
-            pl.BlockSpec((8, 128), lambda i: (0, 0)),
+            pl.BlockSpec(memory_space=pltpu.VMEM),
+            pl.BlockSpec(memory_space=pltpu.VMEM),
         ],
         out_specs=(
             pl.BlockSpec((16, ROWS, COLS * N_MZ), lambda i: (0, 0, 0)),

time: 88.9 us -> 79.8 us (0.90)
  local copies, waits for them, and re-layouts: 6.35 us -> 0.51 us
  Pallas kernels: 81.6 us -> 78.5 us
    unnamed x10 -> x0, local copies, waits for them, and re-layouts: 4.47 us -> none
    pallas_call x1, Pallas kernels: 6.92 us -> 3.49 us  [body(): pl.pallas_call(place_kernel, grid=(PARTS,), out_shape=(jax.ShapeDtypeStru...]
    reshape x2 -> x0, local copies, waits for them, and re-layouts: 1.37 us -> none  [the longest x1 0.68 us: body(): owner.reshape(1, -1)]
where the time goes in v2:
time: 79.8 us; the launch traced here: 79.7 us
  Pallas kernels  78.5 us (98%)
    pallas_call x1, Pallas kernels, body(): pl.pallas_call(produce_kernel, out_shape=(jax.ShapeDtypeStruct((PARTS, N_...  75 us
    pallas_call x1, Pallas kernels, body(): pl.pallas_call(place_kernel, grid=(PARTS,), out_shape=(jax.ShapeDtypeStru...  3.49 us

profile of v2, /device:TPU:11, one launch (start us, length us, event | category | flops | bytes accessed | tf_op | source)
XLA Modules:
  0.0 79.7 jit_solution(7518656794368304708)
XLA Ops:
  0.6 75.0 %shard_map.94 = (bf16[4,16,16,16,128]{4,3,2,1,0:T(8,128)(2,1)S(1)}, f32[8,128]{1,0:T(8,128)S(1)}) custom-call(bf16[8,256,256]{2,1,0:T(8,128)(2,1)} %bitcast.5, s32[384]{0:T(512)} %owner_in.1, s32[4,384]{1,0:T(4,128)} %bitcast.6, s32[384]{0:T(512)} %pattern_index_in.1, f32[4,64]{1,0:T(4,128)} %bitcast.7, bf16[256,640]{1,0:T(8,128)(2,1)} %constant.4.clone.blur_in, ...), custom_call_target="tpu_custom_call" | custom-call | tf_op jit(solution)/shard_map/pallas_call | solution.py:363
  75.7 3.5 %shard_map.95 = (bf16[16,32,1024]{2,1,0:T(8,128)(2,1)}, bf16[48,32,1024]{2,1,0:T(8,128)(2,1)}, f32[8,128]{1,0:T(8,128)S(1)}) custom-call(bf16[4,16,16,16,128]{4,3,2,1,0:T(8,128)(2,1)S(1)} %get-tuple-element.8.parts, f32[8,128]{1,0:T(8,128)S(1)} %get-tuple-element.9.score), custom_call_target="tpu_custom_call" | custom-call | tf_op jit(solution)/shard_map/pallas_call | solution.py:415
  79.2 0.5 slice_bitcast_fusion

commit v3 on v2

v3 whole, which is shorter than its diff:
```python
import math

import jax
import jax.numpy as jnp
import ml_dtypes
import numpy as np
from jax import lax
from jax.experimental import pallas as pl
from jax.experimental.pallas import tpu as pltpu
from jax.sharding import PartitionSpec as P

MESH = pl.DeviceIdType.MESH
F32, BF16 = jnp.float32, jnp.bfloat16

CAP = 48
N_MZ, N_PIX = 16, 8
SIDE = 4
ROWS, COLS, BINS = 32, 64, 256
GROUPS = ROWS // 4
PIXELS = ROWS * COLS
EXTRA = 128
PARTS = 4

gauss_raw = [math.exp(-offset * offset / 4.5) for offset in range(-3, 4)]
taps = [value / sum(gauss_raw) for value in gauss_raw]

ORDER = [(0, 1), (1, 0), (0, 3), (3, 0), (1, 1), (3, 3), (1, 3), (3, 1), (2, 0), (0, 2), (2, 1), (1, 2), (2, 3), (3, 2), (2, 2)]


def tap(offset):
    return taps[offset + 3] if -3 <= offset <= 3 else 0.0


def split(matrix):
    high = matrix.astype(ml_dtypes.bfloat16)
    low = (matrix - high.astype(np.float64)).astype(ml_dtypes.bfloat16)
    return high, low


def constants():
    own = np.zeros((256, 256))
    sides = np.zeros((256, 32))
    pick = np.zeros((32, 256))
    for r in range(4):
        for c in range(COLS):
            for k in range(COLS):
                own[r * COLS + c, r * COLS + k] = tap(k - c)
            for j in range(4):
                sides[r * COLS + c, r * 4 + j] = tap(j - 4 - c)
                sides[r * COLS + c, 16 + r * 4 + j] = tap(COLS + j - c)
        for j in range(4):
            pick[r * 4 + j, r * COLS + j] = 1.0
            pick[16 + r * 4 + j, r * COLS + COLS - 4 + j] = 1.0
    seam = np.zeros((64, 320))
    for r in range(ROWS):
        for k in range(ROWS + 8):
            down = tap(k - 4 - r)
            for j in range(4):
                for edge in range(2):
                    seam[edge * 32 + r, k * 4 + j] = down * tap(j - 4 + 1 - edge)
                    seam[edge * 32 + r, 160 + k * 4 + j] = down * tap(j + 1 - edge)
    own_high, own_low = split(own)
    sides_high, sides_low = split(sides)
    blank = np.zeros((256, 64), ml_dtypes.bfloat16)
    first = np.concatenate([own_high, own_low, sides_high, sides_low, blank], axis=1)
    seam_high, seam_low = split(seam)
    second = np.zeros((96, 640), ml_dtypes.bfloat16)
    second[:64] = np.concatenate([seam_high, seam_low], axis=1)
    second[64:, :256] = pick.astype(ml_dtypes.bfloat16)
    wide = np.zeros((512, 256))
    for strip in range(4):
        for half in range(2):
            for c in range(COLS):
                for k in range(128):
                    wide[strip * 128 + half * COLS + c, half * 128 + k] = tap((strip - 1) * COLS + c - k)
    return first, second, np.concatenate(split(wide), axis=1)


def dot(a, b):
    return jnp.dot(a, b, preferred_element_type=F32)


def dot_nt(a, b):
    return lax.dot_general(a, b, (((1,), (1,)), ((), ())), preferred_element_type=F32)


def iota(shape, axis):
    return lax.broadcasted_iota(jnp.int32, shape, axis)


def rolled_tiles(tiles):
    return jnp.swapaxes(jnp.stack(tiles), 0, 1)


def join_strips(part, target):
    for j in range(N_MZ // 2):
        a, b = part[2 * j], part[2 * j + 1]
        at = slice(j * 128, (j + 1) * 128)
        target[:, 0:16, at] = jnp.concatenate([a[:, :, :64], b[:, :, :64]], axis=2)
        target[:, 16:32, at] = jnp.concatenate([a[:, :, 64:], b[:, :, 64:]], axis=2)


def produce_kernel(
    spectra, owner_in, peaks_in, pattern_index_in, patterns_in, blur_in, more_in, wide_in, done, last, score,
    owner, peaks, pattern_index, patterns, blur, more, wide, xs, pack_left, pack_right, left, right, ys, ion, coef,
    form, out, raw, land, rows_wide, joined, note, notes, total, totals,
    load_sem, halo_send, halo_recv, part_send, part_recv, part_own, rows_send, rows_recv, done_sem,
    note_send, note_recv, total_send, total_recv,
):
    pix, mz = lax.axis_index("pix"), lax.axis_index("mz")
    z, y = mz // SIDE, mz % SIDE

    def device(dp, dm):
        return {"pix": (pix + dp + N_PIX) % N_PIX, "mz": (mz + dm + N_MZ) % N_MZ}

    def peer(dz, dy):
        return ((z + dz) % SIDE) * SIDE + (y + dy) % SIDE

    def remote(src, dst, send, recv, target):
        return pltpu.make_async_remote_copy(
            src_ref=src, dst_ref=dst, send_sem=send, recv_sem=recv, device_id=target, device_id_type=MESH
        )

    sources = [spectra, more_in, blur_in, owner_in, peaks_in, pattern_index_in, patterns_in, wide_in]
    targets = [xs.at[pl.ds(1, GROUPS)], more, blur, owner, peaks, pattern_index, patterns, wide]
    loads = [pltpu.make_async_copy(src, dst, load_sem.at[i]) for i, (src, dst) in enumerate(zip(sources, targets))]
    for copy in loads:
        copy.start()

    barrier = pltpu.get_barrier_semaphore()
    near = [(1, 0), (-1, 0), (1, 1), (1, -1), (-1, 1), (-1, -1)]
    for dz, dy in ORDER:
        pl.semaphore_signal(barrier, inc=1, device_id={"mz": peer(dz, dy)}, device_id_type=MESH)
    for dp, dm in near:
        pl.semaphore_signal(barrier, inc=1, device_id=device(dp, dm), device_id_type=MESH)
    for dp in range(2, N_PIX - 1):
        pl.semaphore_signal(barrier, inc=1, device_id=device(dp, 0), device_id_type=MESH)

    for copy in loads[:2]:
        copy.wait()
    pick = more[64:96, 0:256]
    for g in range(1, GROUPS + 1):
        ends = dot(pick, xs[g]).astype(BF16)
        pack_left[g] = ends[0:16]
        pack_right[g] = ends[16:32]
    same = (iota((BINS, BINS), 0) == iota((BINS, BINS), 1)).astype(F32).astype(BF16)
    tiles = []
    for n in range(8):
        rows_here = [xs[1 + r // 4, (r % 4) * COLS : (r % 4 + 1) * COLS, :] for r in (2 * n, 2 * n + 16, 2 * n + 1, 2 * n + 17)]
        turned = dot_nt(same, jnp.concatenate(rows_here, axis=0)).astype(BF16)
        tiles += [turned[:, 0:128], turned[:, 128:256]]
    for d in range(N_MZ):
        out[0, d] = rolled_tiles([tile[d * 16 : (d + 1) * 16] for tile in tiles])

    pl.semaphore_wait(barrier, len(ORDER) + len(near) + N_PIX - 3)

    inner = pl.ds(1, GROUPS)
    halo = [
        (xs.at[GROUPS], xs.at[0], (1, 0)),
        (xs.at[1], xs.at[GROUPS + 1], (-1, 0)),
        (pack_right.at[inner], left.at[inner], (0, 1)),
        (pack_left.at[inner], right.at[inner], (0, -1)),
        (pack_right.at[GROUPS], left.at[0], (1, 1)),
        (pack_right.at[1], left.at[GROUPS + 1], (-1, 1)),
        (pack_left.at[GROUPS], right.at[0], (1, -1)),
        (pack_left.at[1], right.at[GROUPS + 1], (-1, -1)),
    ]
    halo = [
        remote(src, dst, halo_send.at[i], halo_recv.at[i], device(*to)) for i, (src, dst, to) in enumerate(halo)
    ]
    for copy in halo:
        copy.start()

    def send(q, target):
        copies = []
        for i, (dz, dy) in enumerate(ORDER):
            to = peer(dz, dy)
            copies.append(remote(out.at[q, to], target.at[mz], part_send.at[q, i], part_recv.at[q, i], {"mz": to}))
        copies.append(pltpu.make_async_copy(out.at[q, mz], target.at[mz], part_own.at[q]))
        for copy in copies:
            copy.start()
        return copies

    sent_raw = send(0, raw)

    loads[2].wait()
    blur_high, blur_low, blur_sides = blur[:, 0:256], blur[:, 256:512], blur[:, 512:576]

    def columns_own(g):
        ys[g] = dot(blur_high, xs[g]) + dot(blur_low, xs[g])

    for g in range(1, GROUPS + 1):
        columns_own(g)

    for copy in loads[3:]:
        copy.wait()
    count = owner.shape[0]
    owner_row = owner[...].reshape(1, count)
    owner_hot = (iota((N_MZ, count), 0) == owner_row).astype(F32)
    before = (iota((count, count), 0) < iota((count, count), 1)).astype(F32).astype(BF16)
    earlier = dot(owner_hot.astype(BF16), before)
    rank = jnp.sum(earlier * owner_hot, axis=0, keepdims=True)
    slot = owner_row * CAP + rank.astype(jnp.int32)
    pattern_hot = (iota((patterns.shape[1], count), 0) == pattern_index[...].reshape(1, count)).astype(F32).astype(BF16)
    weight = dot(patterns[...].astype(BF16), pattern_hot)
    spread = jnp.zeros((BINS, count), F32)
    for k in range(peaks.shape[0]):
        spread += jnp.where(iota((BINS, count), 0) == peaks[k : k + 1, :], weight[k : k + 1, :], 0.0)
    spread = spread.astype(BF16)
    place = iota((256, count), 0)
    place = (place // 16) * CAP + place % 16
    for q in range(1, PARTS):
        slot_hot = (place + (q - 1) * 16 == slot).astype(F32).astype(BF16)
        coef[q - 1] = dot_nt(slot_hot, spread).astype(BF16)

    for copy in halo:
        copy.wait()

    @pl.when(pix == 0)
    def _():
        xs[0] = jnp.zeros(xs.shape[1:], BF16)
        left[0] = jnp.zeros(left.shape[1:], BF16)
        right[0] = jnp.zeros(right.shape[1:], BF16)

    @pl.when(pix == N_PIX - 1)
    def _():
        xs[GROUPS + 1] = jnp.zeros(xs.shape[1:], BF16)
        left[GROUPS + 1] = jnp.zeros(left.shape[1:], BF16)
        right[GROUPS + 1] = jnp.zeros(right.shape[1:], BF16)

    @pl.when(mz == 0)
    def _():
        left[...] = jnp.zeros(left.shape, BF16)

    @pl.when(mz == N_MZ - 1)
    def _():
        right[...] = jnp.zeros(right.shape, BF16)

    columns_own(0)
    columns_own(GROUPS + 1)
    for g in range(GROUPS + 2):
        sides = jnp.concatenate([left[g], right[g], left[g], right[g]], axis=0)
        ys[g] += dot(blur_sides, sides)

    for g in (0, GROUPS + 1):
        pack_left[g] = dot(pick[0:16], xs[g]).astype(BF16)
    edge = jnp.concatenate([left[...].reshape(160, BINS), pack_left[...].reshape(160, BINS)], axis=0)
    ion[PIXELS + 64 : PIXELS + 128] = (dot(more[0:64, 0:320], edge) + dot(more[0:64, 320:640], edge)).astype(BF16)

    def rows(c, carry):
        for lanes in (slice(0, 128), slice(128, 256)):
            lines = [ys[k // 4, pl.ds(pl.multiple_of((k % 4) * COLS + c * 16, 16), 16), lanes] for k in range(ROWS + 7)]
            for r in range(-1, ROWS):
                result = taps[3] * lines[r + 4]
                for i in range(3):
                    result = result + taps[i] * (lines[r + 1 + i] + lines[r + 7 - i])
                at = PIXELS if r < 0 else (r % 16) * 128 + (r // 16) * 64
                ion[pl.ds(pl.multiple_of(at + c * 16, 16), 16), lanes] = result.astype(BF16)
        return carry

    lax.fori_loop(0, COLS // 16, rows, 0)

    def product(q):
        tiles = []
        for n in range(PIXELS // 256):
            result = dot_nt(coef[q - 1], ion[n * 256 : (n + 1) * 256, :]).astype(BF16)
            tiles += [result[:, 0:128], result[:, 128:256]]
        for j, tile in enumerate(tiles):
            form[q - 1, j] = tile
        form[q - 1, 16] = dot_nt(coef[q - 1], ion[PIXELS : PIXELS + 128, :]).astype(BF16)
        for d in range(N_MZ):
            out[q, d] = rolled_tiles([tile[d * 16 : (d + 1) * 16] for tile in tiles])

    product(1)
    sent_1 = send(1, land.at[0])
    product(2)
    product(3)

    lane, sub = iota((64, 128), 1), iota((8, 128), 0)
    keep_across = (lane % 64 != 0).astype(F32)
    keep_seam = jnp.where(mz > 0, (lane >= 96).astype(F32), 0.0)
    keep_top = jnp.where(pix > 0, 1.0, jnp.where(lane < 64, 0.0, 1.0))
    note[...] = jnp.zeros(note.shape, F32)

    for q in range(1, PARTS):
        def scores(d, carry, q=q):
            def value(j):
                return form[q - 1, j, pl.ds(pl.multiple_of(d * 64, 64), 64), :].astype(F32)

            extra = value(16)
            prior = jnp.where(lane < 64, extra, pltpu.roll(value(15), 64, 1))
            across = jnp.zeros((64, 128), F32)
            down = jnp.zeros((64, 128), F32)
            energy = jnp.zeros((64, 128), F32)
            for j in range(16):
                now = value(j)
                step = now - pltpu.roll(now, 1, 1)
                across += step * step
                step = now - prior
                if j == 0:
                    step = step * keep_top
                down += step * step
                energy += now * now
                prior = now
            step = extra - pltpu.roll(extra, 32, 1)
            rough = across * keep_across + down + step * step * keep_seam
            rough = jnp.sum(rough, axis=1, keepdims=True)
            energy = jnp.sum(energy, axis=1, keepdims=True)
            for k in range(4):
                acc = jnp.zeros((8, 128), F32)
                for half in range(2):
                    at = k * 16 + half * 8
                    base = sub + ((q - 1) * 16 + half * 8)
                    acc += jnp.where(lane[0:8] == base, rough[at : at + 8], 0.0)
                    acc += jnp.where(lane[0:8] == base + 64, energy[at : at + 8], 0.0)
                note[d * 4 + k] += acc
            return carry

        lax.fori_loop(0, N_MZ // 4, scores, 0)

    small = []
    for i, (dz, dy) in enumerate(ORDER):
        to = peer(dz, dy)
        small.append(remote(note.at[to], notes.at[mz], note_send.at[i], note_recv.at[i], {"mz": to}))
    for copy in small:
        copy.start()
    sent_2 = send(2, land.at[1])

    for copy in sent_raw:
        copy.wait()
    blank = jnp.zeros((256, 128), BF16)
    for j in range(N_MZ // 2):
        strips = [raw[k].reshape(256, 128) if 0 <= k < N_MZ else blank for k in range(2 * j - 1, 2 * j + 3)]
        strips = jnp.concatenate(strips, axis=1)
        result = (dot(strips, wide[:, 0:256]) + dot(strips, wide[:, 256:512])).reshape(16, 16, 256)
        rows_wide[:, 8:24, j * 128 : (j + 1) * 128] = result[:, :, 0:128]
        rows_wide[:, 24:40, j * 128 : (j + 1) * 128] = result[:, :, 128:256]
    above, below = pl.ds(0, 8), pl.ds(40, 8)
    edges = [
        remote(rows_wide.at[:, pl.ds(32, 8)], rows_wide.at[:, above], rows_send.at[0], rows_recv.at[0], device(1, 0)),
        remote(rows_wide.at[:, pl.ds(8, 8)], rows_wide.at[:, below], rows_send.at[1], rows_recv.at[1], device(-1, 0)),
    ]
    for copy in edges:
        copy.start()

    for copy in small:
        copy.wait()
    notes[mz] = note[mz]
    total[...] = jnp.sum(notes[...], axis=0)
    small = []
    for dp in range(1, N_PIX):
        to = device(dp, 0)
        small.append(remote(total, totals.at[pix], total_send.at[dp], total_recv.at[dp], to))
    for copy in small:
        copy.start()
    sent_3 = send(3, last)

    for copy in edges:
        copy.wait()

    @pl.when(pix == 0)
    def _():
        rows_wide[:, above, :] = jnp.zeros((16, 8, COLS * N_MZ), F32)

    @pl.when(pix == N_PIX - 1)
    def _():
        rows_wide[:, below, :] = jnp.zeros((16, 8, COLS * N_MZ), F32)

    def own_rows(b, carry):
        for j in range(N_MZ // 2):
            x = rows_wide[b, :, j * 128 : (j + 1) * 128]
            result = taps[3] * x[8:40]
            for i in range(3):
                result = result + taps[i] * (x[5 + i : 37 + i] + x[11 - i : 43 - i])
            joined[b, :, j * 128 : (j + 1) * 128] = result.astype(BF16)
        return carry

    lax.fori_loop(0, 16, own_rows, 0)
    stores = [pltpu.make_async_copy(joined.at[pl.ds(0, 16)], done.at[pl.ds(0, 16)], done_sem.at[0])]
    stores[0].start()

    for copy in small:
        copy.wait()
    totals[pix] = total[...]
    final = jnp.sum(jnp.sum(totals[...], axis=0), axis=0, keepdims=True)
    final = final / (pltpu.roll(final, 64, 1) + 1e-5)
    score[...] = jnp.broadcast_to(final, (8, 128))

    for q, copies in ((1, sent_1), (2, sent_2)):
        for copy in copies:
            copy.wait()
        at = pl.ds(q * 16, 16)
        join_strips(land.at[q - 1], joined.at[at])
        stores.append(pltpu.make_async_copy(joined.at[at], done.at[at], done_sem.at[q]))
        stores[q].start()
    for copy in stores + sent_3:
        copy.wait()


def place_kernel(done, last, score, ion_out, form_out, chaos_out, joined, sems):
    copies = [
        pltpu.make_async_copy(done.at[pl.ds(0, 16)], ion_out, sems.at[0]),
        pltpu.make_async_copy(done.at[pl.ds(16, 32)], form_out.at[pl.ds(0, 32)], sems.at[1]),
        pltpu.make_async_copy(joined, form_out.at[pl.ds(32, 16)], sems.at[2]),
    ]
    copies[0].start()
    copies[1].start()
    join_strips(last, joined)
    copies[2].start()
    chaos_out[...] = score[...]
    for copy in copies:
        copy.wait()


def body(spectra, owner, peaks, pattern_index, patterns):
    first, second, third = constants()
    dma = pltpu.SemaphoreType.DMA
    vmem, hbm, free = (pl.BlockSpec(memory_space=space) for space in (pltpu.VMEM, pltpu.HBM, pl.ANY))
    peers = len(ORDER)
    wide_cols = COLS * N_MZ
    inputs = (
        spectra.reshape(GROUPS, 256, BINS), owner, peaks.T, pattern_index, patterns.T,
        jnp.asarray(first), jnp.asarray(second), jnp.asarray(third),
    )
    inputs = [pltpu.with_memory_space_constraint(x, pltpu.HBM) for x in inputs]
    done, last, score = pl.pallas_call(
        produce_kernel,
        out_shape=(
            jax.ShapeDtypeStruct((48, ROWS, wide_cols), BF16),
            jax.ShapeDtypeStruct((N_MZ, 16, 16, 128), BF16),
            jax.ShapeDtypeStruct((8, 128), F32),
        ),
        in_specs=[hbm] * len(inputs),
        out_specs=(free, free, vmem),
        scratch_shapes=[pltpu.VMEM(x.shape, x.dtype) for x in inputs[1:]]
        + [
            pltpu.VMEM((GROUPS + 2, 256, BINS), BF16),
            pltpu.VMEM((GROUPS + 2, 16, BINS), BF16),
            pltpu.VMEM((GROUPS + 2, 16, BINS), BF16),
            pltpu.VMEM((GROUPS + 2, 16, BINS), BF16),
            pltpu.VMEM((GROUPS + 2, 16, BINS), BF16),
            pltpu.VMEM((GROUPS + 2, 256, BINS), F32),
            pltpu.VMEM((PIXELS + EXTRA, BINS), BF16),
            pltpu.VMEM((PARTS - 1, 256, BINS), BF16),
            pltpu.VMEM((PARTS - 1, 17, 256, 128), BF16),
            pltpu.VMEM((PARTS, N_MZ, 16, 16, 128), BF16),
            pltpu.VMEM((N_MZ, 16, 16, 128), BF16),
            pltpu.VMEM((2, N_MZ, 16, 16, 128), BF16),
            pltpu.VMEM((16, ROWS + 16, wide_cols), F32),
            pltpu.VMEM((48, ROWS, wide_cols), BF16),
            pltpu.VMEM((N_MZ, 8, 128), F32),
            pltpu.VMEM((N_MZ, 8, 128), F32),
            pltpu.VMEM((8, 128), F32),
            pltpu.VMEM((N_PIX, 8, 128), F32),
            dma((len(inputs),)),
            dma((8,)),
            dma((8,)),
            dma((PARTS, peers)),
            dma((PARTS, peers)),
            dma((PARTS,)),
            dma((2,)),
            dma((2,)),
            dma((3,)),
            dma((peers,)),
            dma((peers,)),
            dma((N_PIX,)),
            dma((N_PIX,)),
        ],
        compiler_params=pltpu.CompilerParams(
            collective_id=0, has_side_effects=True, vmem_limit_bytes=48 * 2**20
        ),
    )(*inputs)
    ion_images, formula_images, chaos = pl.pallas_call(
        place_kernel,
        out_shape=(
            jax.ShapeDtypeStruct((16, ROWS, wide_cols), BF16),
            jax.ShapeDtypeStruct((CAP, ROWS, wide_cols), BF16),
            jax.ShapeDtypeStruct((8, 128), F32),
        ),
        in_specs=[vmem, vmem, vmem],
        out_specs=(free, free, vmem),
        scratch_shapes=[pltpu.VMEM((16, ROWS, wide_cols), BF16), dma((3,))],
        compiler_params=pltpu.CompilerParams(vmem_limit_bytes=32 * 2**20),
    )(done, last, score)
    return ion_images, formula_images, chaos[0, :CAP]


def solution(mesh):
    in_specs = (P("pix", "mz", None), P(), P(), P(), P())
    out_specs = (P("mz", "pix", None), P("mz", "pix", None), P("mz"))
    return jax.shard_map(body, mesh=mesh, in_specs=in_specs, out_specs=out_specs, check_vma=False)
```

time: 79.8 us -> 64 us (0.80)
  the two profiles are of different devices: /device:TPU:11 before, /device:TPU:1 now
where the time goes in v3:
time: 64 us; the launch traced here: 63.9 us
  Pallas kernels  62.7 us (98%)
  between operations  0.65 us (1%)
    pallas_call x1, Pallas kernels, body(): pl.pallas_call(produce_kernel, out_shape=(jax.ShapeDtypeStruct((48, ROWS,...  60.7 us
    pallas_call x1, Pallas kernels, body(): pl.pallas_call(place_kernel, out_shape=(jax.ShapeDtypeStruct((16, ROWS, w...  2.03 us

profile of v3, /device:TPU:1, one launch (start us, length us, event | category | flops | bytes accessed | tf_op | source)
XLA Modules:
  0.0 63.9 jit_solution(8985730545748202387)
XLA Ops:
  0.6 60.7 %shard_map.103 = (bf16[48,32,1024]{2,1,0:T(8,128)(2,1)S(1)}, bf16[16,16,16,128]{3,2,1,0:T(8,128)(2,1)S(1)}, f32[8,128]{1,0:T(8,128)S(1)}) custom-call(bf16[8,256,256]{2,1,0:T(8,128)(2,1)} %bitcast.5, s32[384]{0:T(512)} %owner_in.1, s32[4,384]{1,0:T(4,128)} %bitcast.6, s32[384]{0:T(512)} %pattern_index_in.1, f32[4,64]{1,0:T(4,128)} %bitcast.7, ...), custom_call_target="tpu_custom_call" | custom-call | tf_op jit(solution)/shard_map/pallas_call | solution.py:426
  61.3 2.0 %shard_map.104 = (bf16[16,32,1024]{2,1,0:T(8,128)(2,1)}, bf16[48,32,1024]{2,1,0:T(8,128)(2,1)}, f32[8,128]{1,0:T(8,128)S(1)}) custom-call(bf16[48,32,1024]{2,1,0:T(8,128)(2,1)S(1)} %get-tuple-element.9.done, bf16[16,16,16,128]{3,2,1,0:T(8,128)(2,1)S(1)} %get-tuple-element.10.last, f32[8,128]{1,0:T(8,128)S(1)} %get-tuple-element.11.score), custom_call_target="tpu_custom_call" | custom-call | tf_op jit(solution)/shard_map/pallas_call | solution.py:473
  63.4 0.5 slice_bitcast_fusion

commit v4 on v3

--- a/solution.py
+++ b/solution.py
@@ -20,6 +20,7 @@
 PIXELS = ROWS * COLS
 EXTRA = 128
 PARTS = 4
+TURNED = (0, 0, 0, 0)
 
 gauss_raw = [math.exp(-offset * offset / 4.5) for offset in range(-3, 4)]
 taps = [value / sum(gauss_raw) for value in gauss_raw]
@@ -121,6 +122,9 @@
             src_ref=src, dst_ref=dst, send_sem=send, recv_sem=recv, device_id=target, device_id_type=MESH
         )
 
+    def slot_of(g):
+        return {0: 0, GROUPS + 1: 1}.get(g, g + 1)
+
     sources = [spectra, more_in, blur_in, owner_in, peaks_in, pattern_index_in, patterns_in, wide_in]
     targets = [xs.at[pl.ds(1, GROUPS)], more, blur, owner, peaks, pattern_index, patterns, wide]
     loads = [pltpu.make_async_copy(src, dst, load_sem.at[i]) for i, (src, dst) in enumerate(zip(sources, targets))]
@@ -128,21 +132,22 @@
         copy.start()
 
     barrier = pltpu.get_barrier_semaphore()
-    near = [(1, 0), (-1, 0), (1, 1), (1, -1), (-1, 1), (-1, -1)]
     for dz, dy in ORDER:
         pl.semaphore_signal(barrier, inc=1, device_id={"mz": peer(dz, dy)}, device_id_type=MESH)
-    for dp, dm in near:
-        pl.semaphore_signal(barrier, inc=1, device_id=device(dp, dm), device_id_type=MESH)
-    for dp in range(2, N_PIX - 1):
+    for dp in (1, 7, 2, 3, 4, 5, 6):
         pl.semaphore_signal(barrier, inc=1, device_id=device(dp, 0), device_id_type=MESH)
 
     for copy in loads[:2]:
         copy.wait()
     pick = more[64:96, 0:256]
+
+    def pack(g):
+        ends = dot(pick, xs[g]).astype(BF16)
+        pack_left[slot_of(g)] = ends[0:16]
+        pack_right[slot_of(g)] = ends[16:32]
+
     for g in range(1, GROUPS + 1):
-        ends = dot(pick, xs[g]).astype(BF16)
-        pack_left[g] = ends[0:16]
-        pack_right[g] = ends[16:32]
+        pack(g)
     same = (iota((BINS, BINS), 0) == iota((BINS, BINS), 1)).astype(F32).astype(BF16)
     tiles = []
     for n in range(8):
@@ -152,36 +157,44 @@
     for d in range(N_MZ):
         out[0, d] = rolled_tiles([tile[d * 16 : (d + 1) * 16] for tile in tiles])
 
-    pl.semaphore_wait(barrier, len(ORDER) + len(near) + N_PIX - 3)
-
-    inner = pl.ds(1, GROUPS)
+    pl.semaphore_wait(barrier, len(ORDER) + N_PIX - 1)
+
+    inner, outer = pl.ds(2, GROUPS), pl.ds(0, 2)
     halo = [
         (xs.at[GROUPS], xs.at[0], (1, 0)),
         (xs.at[1], xs.at[GROUPS + 1], (-1, 0)),
         (pack_right.at[inner], left.at[inner], (0, 1)),
         (pack_left.at[inner], right.at[inner], (0, -1)),
-        (pack_right.at[GROUPS], left.at[0], (1, 1)),
-        (pack_right.at[1], left.at[GROUPS + 1], (-1, 1)),
-        (pack_left.at[GROUPS], right.at[0], (1, -1)),
-        (pack_left.at[1], right.at[GROUPS + 1], (-1, -1)),
+        (pack_right.at[outer], left.at[outer], (0, 1)),
+        (pack_left.at[outer], right.at[outer], (0, -1)),
     ]
     halo = [
         remote(src, dst, halo_send.at[i], halo_recv.at[i], device(*to)) for i, (src, dst, to) in enumerate(halo)
     ]
-    for copy in halo:
+    for copy in halo[:4]:
         copy.start()
 
-    def send(q, target):
+    def all_of(ref, sem, count):
+        block = ref.at[pl.ds(0, count)]
+        pltpu.make_async_copy(block, block, sem).wait()
+
+    def wait_part(q, target):
+        all_of(target, part_recv.at[q], len(ORDER))
+        all_of(out.at[q], part_send.at[q], len(ORDER))
+        pltpu.make_async_copy(out.at[q, mz], target.at[mz], part_own.at[q]).wait()
+
+    def send(q, target, begin, end):
         copies = []
-        for i, (dz, dy) in enumerate(ORDER):
+        order = list(enumerate(ORDER))
+        for i, (dz, dy) in (order[::-1] if TURNED[q] else order)[begin:end]:
             to = peer(dz, dy)
-            copies.append(remote(out.at[q, to], target.at[mz], part_send.at[q, i], part_recv.at[q, i], {"mz": to}))
-        copies.append(pltpu.make_async_copy(out.at[q, mz], target.at[mz], part_own.at[q]))
+            copies.append(remote(out.at[q, to], target.at[mz], part_send.at[q], part_recv.at[q], {"mz": to}))
+        if begin == 0:
+            copies.append(pltpu.make_async_copy(out.at[q, mz], target.at[mz], part_own.at[q]))
         for copy in copies:
             copy.start()
-        return copies
-
-    sent_raw = send(0, raw)
+
+    send(0, raw, 0, 8)
 
     loads[2].wait()
     blur_high, blur_low, blur_sides = blur[:, 0:256], blur[:, 256:512], blur[:, 512:576]
@@ -213,20 +226,26 @@
         slot_hot = (place + (q - 1) * 16 == slot).astype(F32).astype(BF16)
         coef[q - 1] = dot_nt(slot_hot, spread).astype(BF16)
 
-    for copy in halo:
+    for copy in halo[:2]:
         copy.wait()
 
     @pl.when(pix == 0)
     def _():
         xs[0] = jnp.zeros(xs.shape[1:], BF16)
-        left[0] = jnp.zeros(left.shape[1:], BF16)
-        right[0] = jnp.zeros(right.shape[1:], BF16)
 
     @pl.when(pix == N_PIX - 1)
     def _():
         xs[GROUPS + 1] = jnp.zeros(xs.shape[1:], BF16)
-        left[GROUPS + 1] = jnp.zeros(left.shape[1:], BF16)
-        right[GROUPS + 1] = jnp.zeros(right.shape[1:], BF16)
+
+    pack(0)
+    pack(GROUPS + 1)
+    for copy in halo[4:]:
+        copy.start()
+    send(0, raw, 8, 15)
+    columns_own(0)
+    columns_own(GROUPS + 1)
+    for copy in halo[2:]:
+        copy.wait()
 
     @pl.when(mz == 0)
     def _():
@@ -236,15 +255,13 @@
     def _():
         right[...] = jnp.zeros(right.shape, BF16)
 
-    columns_own(0)
-    columns_own(GROUPS + 1)
     for g in range(GROUPS + 2):
-        sides = jnp.concatenate([left[g], right[g], left[g], right[g]], axis=0)
+        at = slot_of(g)
+        sides = jnp.concatenate([left[at], right[at], left[at], right[at]], axis=0)
         ys[g] += dot(blur_sides, sides)
 
-    for g in (0, GROUPS + 1):
-        pack_left[g] = dot(pick[0:16], xs[g]).astype(BF16)
-    edge = jnp.concatenate([left[...].reshape(160, BINS), pack_left[...].reshape(160, BINS)], axis=0)
+    edge = [ref[slot_of(g)] for ref in (left, pack_left) for g in range(GROUPS + 2)]
+    edge = jnp.concatenate(edge, axis=0)
     ion[PIXELS + 64 : PIXELS + 128] = (dot(more[0:64, 0:320], edge) + dot(more[0:64, 320:640], edge)).astype(BF16)
 
     def rows(c, carry):
@@ -272,7 +289,7 @@
             out[q, d] = rolled_tiles([tile[d * 16 : (d + 1) * 16] for tile in tiles])
 
     product(1)
-    sent_1 = send(1, land.at[0])
+    send(1, land.at[0], 0, 8)
     product(2)
     product(3)
 
@@ -313,7 +330,7 @@
                     base = sub + ((q - 1) * 16 + half * 8)
                     acc += jnp.where(lane[0:8] == base, rough[at : at + 8], 0.0)
                     acc += jnp.where(lane[0:8] == base + 64, energy[at : at + 8], 0.0)
-                note[d * 4 + k] += acc
+                note[d * 4 + k] += jnp.sum(acc, axis=0, keepdims=True)
             return carry
 
         lax.fori_loop(0, N_MZ // 4, scores, 0)
@@ -321,13 +338,13 @@
     small = []
     for i, (dz, dy) in enumerate(ORDER):
         to = peer(dz, dy)
-        small.append(remote(note.at[to], notes.at[mz], note_send.at[i], note_recv.at[i], {"mz": to}))
+        small.append(remote(note.at[to], notes.at[mz], note_send, note_recv, {"mz": to}))
     for copy in small:
         copy.start()
-    sent_2 = send(2, land.at[1])
-
-    for copy in sent_raw:
-        copy.wait()
+    send(1, land.at[0], 8, 15)
+    send(2, land.at[1], 0, 15)
+
+    wait_part(0, raw)
     blank = jnp.zeros((256, 128), BF16)
     for j in range(N_MZ // 2):
         strips = [raw[k].reshape(256, 128) if 0 <= k < N_MZ else blank for k in range(2 * j - 1, 2 * j + 3)]
@@ -343,17 +360,19 @@
     for copy in edges:
         copy.start()
 
-    for copy in small:
-        copy.wait()
+
+    all_of(notes, note_recv, len(ORDER))
+    all_of(note, note_send, len(ORDER))
     notes[mz] = note[mz]
     total[...] = jnp.sum(notes[...], axis=0)
     small = []
     for dp in range(1, N_PIX):
         to = device(dp, 0)
-        small.append(remote(total, totals.at[pix], total_send.at[dp], total_recv.at[dp], to))
+        small.append(remote(total, totals.at[pix], total_send, total_recv, to))
     for copy in small:
         copy.start()
-    sent_3 = send(3, last)
+    send(2, land.at[1], 15, 15)
+    send(3, last, 0, 15)
 
     for copy in edges:
         copy.wait()
@@ -379,22 +398,22 @@
     stores = [pltpu.make_async_copy(joined.at[pl.ds(0, 16)], done.at[pl.ds(0, 16)], done_sem.at[0])]
     stores[0].start()
 
-    for copy in small:
-        copy.wait()
+    all_of(totals, total_recv, N_PIX - 1)
+    all_of(totals, total_send, N_PIX - 1)
     totals[pix] = total[...]
-    final = jnp.sum(jnp.sum(totals[...], axis=0), axis=0, keepdims=True)
+    final = jnp.sum(totals[...], axis=0)
     final = final / (pltpu.roll(final, 64, 1) + 1e-5)
     score[...] = jnp.broadcast_to(final, (8, 128))
 
-    for q, copies in ((1, sent_1), (2, sent_2)):
-        for copy in copies:
-            copy.wait()
+    for q in (1, 2):
+        wait_part(q, land.at[q - 1])
         at = pl.ds(q * 16, 16)
         join_strips(land.at[q - 1], joined.at[at])
         stores.append(pltpu.make_async_copy(joined.at[at], done.at[at], done_sem.at[q]))
         stores[q].start()
-    for copy in stores + sent_3:
-        copy.wait()
+    for copy in stores:
+        copy.wait()
+    wait_part(3, last)
 
 
 def place_kernel(done, last, score, ion_out, form_out, chaos_out, joined, sems):
@@ -416,7 +435,6 @@
     first, second, third = constants()
     dma = pltpu.SemaphoreType.DMA
     vmem, hbm, free = (pl.BlockSpec(memory_space=space) for space in (pltpu.VMEM, pltpu.HBM, pl.ANY))
-    peers = len(ORDER)
     wide_cols = COLS * N_MZ
     inputs = (
         spectra.reshape(GROUPS, 256, BINS), owner, peaks.T, pattern_index, patterns.T,
@@ -448,23 +466,23 @@
             pltpu.VMEM((2, N_MZ, 16, 16, 128), BF16),
             pltpu.VMEM((16, ROWS + 16, wide_cols), F32),
             pltpu.VMEM((48, ROWS, wide_cols), BF16),
-            pltpu.VMEM((N_MZ, 8, 128), F32),
-            pltpu.VMEM((N_MZ, 8, 128), F32),
-            pltpu.VMEM((8, 128), F32),
-            pltpu.VMEM((N_PIX, 8, 128), F32),
+            pltpu.VMEM((N_MZ, 1, 128), F32),
+            pltpu.VMEM((N_MZ, 1, 128), F32),
+            pltpu.VMEM((1, 128), F32),
+            pltpu.VMEM((N_PIX, 1, 128), F32),
             dma((len(inputs),)),
-            dma((8,)),
-            dma((8,)),
-            dma((PARTS, peers)),
-            dma((PARTS, peers)),
+            dma((6,)),
+            dma((6,)),
+            dma((PARTS,)),
+            dma((PARTS,)),
             dma((PARTS,)),
             dma((2,)),
             dma((2,)),
             dma((3,)),
-            dma((peers,)),
-            dma((peers,)),
-            dma((N_PIX,)),
-            dma((N_PIX,)),
+            dma,
+            dma,
+            dma,
+            dma,
         ],
         compiler_params=pltpu.CompilerParams(
             collective_id=0, has_side_effects=True, vmem_limit_bytes=48 * 2**20

time: 64 us -> 62 us (0.969)
  Pallas kernels: 62.7 us -> 60.7 us
    pallas_call x1, Pallas kernels: 60.7 us -> 58.6 us  [body(): pl.pallas_call(produce_kernel, out_shape=(jax.ShapeDtypeStruct((48, ROWS,...]
where the time goes in v4:
time: 62 us; the launch traced here: 61.8 us
  Pallas kernels  60.7 us (98%)
  between operations  0.65 us (1%)
    pallas_call x1, Pallas kernels, body(): pl.pallas_call(produce_kernel, out_shape=(jax.ShapeDtypeStruct((48, ROWS,...  58.6 us
    pallas_call x1, Pallas kernels, body(): pl.pallas_call(place_kernel, out_shape=(jax.ShapeDtypeStruct((16, ROWS, w...  2.03 us

profile of v4, /device:TPU:1, one launch (start us, length us, event | category | flops | bytes accessed | tf_op | source)
XLA Modules:
  0.0 61.8 jit_solution(18223350907485834957)
XLA Ops:
  0.6 58.6 %shard_map.103 = (bf16[48,32,1024]{2,1,0:T(8,128)(2,1)S(1)}, bf16[16,16,16,128]{3,2,1,0:T(8,128)(2,1)S(1)}, f32[8,128]{1,0:T(8,128)S(1)}) custom-call(bf16[8,256,256]{2,1,0:T(8,128)(2,1)} %bitcast.5, s32[384]{0:T(512)} %owner_in.1, s32[4,384]{1,0:T(4,128)} %bitcast.6, s32[384]{0:T(512)} %pattern_index_in.1, f32[4,64]{1,0:T(4,128)} %bitcast.7, ...), custom_call_target="tpu_custom_call" | custom-call | tf_op jit(solution)/shard_map/pallas_call | solution.py:444
  59.3 2.0 %shard_map.104 = (bf16[16,32,1024]{2,1,0:T(8,128)(2,1)}, bf16[48,32,1024]{2,1,0:T(8,128)(2,1)}, f32[8,128]{1,0:T(8,128)S(1)}) custom-call(bf16[48,32,1024]{2,1,0:T(8,128)(2,1)S(1)} %get-tuple-element.9.done, bf16[16,16,16,128]{3,2,1,0:T(8,128)(2,1)S(1)} %get-tuple-element.10.last, f32[8,128]{1,0:T(8,128)S(1)} %get-tuple-element.11.score), custom_call_target="tpu_custom_call" | custom-call | tf_op jit(solution)/shard_map/pallas_call | solution.py:491
  61.3 0.5 slice_bitcast_fusion

commit v5 on v4

--- a/solution.py
+++ b/solution.py
@@ -20,7 +20,7 @@
 PIXELS = ROWS * COLS
 EXTRA = 128
 PARTS = 4
-TURNED = (0, 0, 0, 0)
+TURNED = (0, 0, 0, 1)
 
 gauss_raw = [math.exp(-offset * offset / 4.5) for offset in range(-3, 4)]
 taps = [value / sum(gauss_raw) for value in gauss_raw]
@@ -416,17 +416,18 @@
     wait_part(3, last)
 
 
-def place_kernel(done, last, score, ion_out, form_out, chaos_out, joined, sems):
+def place_kernel(done, last, score, ion_out, form_out, chaos_out, joined, chaos, sems):
+    chaos[...] = score[0, 0:CAP]
     copies = [
         pltpu.make_async_copy(done.at[pl.ds(0, 16)], ion_out, sems.at[0]),
         pltpu.make_async_copy(done.at[pl.ds(16, 32)], form_out.at[pl.ds(0, 32)], sems.at[1]),
+        pltpu.make_async_copy(chaos, chaos_out, sems.at[3]),
         pltpu.make_async_copy(joined, form_out.at[pl.ds(32, 16)], sems.at[2]),
     ]
-    copies[0].start()
-    copies[1].start()
+    for copy in copies[:3]:
+        copy.start()
     join_strips(last, joined)
-    copies[2].start()
-    chaos_out[...] = score[...]
+    copies[3].start()
     for copy in copies:
         copy.wait()
 
@@ -493,14 +494,14 @@
         out_shape=(
             jax.ShapeDtypeStruct((16, ROWS, wide_cols), BF16),
             jax.ShapeDtypeStruct((CAP, ROWS, wide_cols), BF16),
-            jax.ShapeDtypeStruct((8, 128), F32),
+            jax.ShapeDtypeStruct((CAP,), F32),
         ),
         in_specs=[vmem, vmem, vmem],
-        out_specs=(free, free, vmem),
-        scratch_shapes=[pltpu.VMEM((16, ROWS, wide_cols), BF16), dma((3,))],
+        out_specs=(free, free, free),
+        scratch_shapes=[pltpu.VMEM((16, ROWS, wide_cols), BF16), pltpu.VMEM((CAP,), F32), dma((4,))],
         compiler_params=pltpu.CompilerParams(vmem_limit_bytes=32 * 2**20),
     )(done, last, score)
-    return ion_images, formula_images, chaos[0, :CAP]
+    return ion_images, formula_images, chaos
 
 
 def solution(mesh):

time: 62 us -> 60.7 us (0.979)
  Pallas kernels: 60.7 us -> 59.8 us
    pallas_call x1, Pallas kernels: 58.6 us -> 57.8 us  [body(): pl.pallas_call(produce_kernel, out_shape=(jax.ShapeDtypeStruct((48, ROWS,...]
where the time goes in v5:
time: 60.7 us; the launch traced here: 60.4 us
  Pallas kernels  59.8 us (99%)
  between operations  0.64 us (1%)
    pallas_call x1, Pallas kernels, body(): pl.pallas_call(produce_kernel, out_shape=(jax.ShapeDtypeStruct((48, ROWS,...  57.8 us
    pallas_call x1, Pallas kernels, body(): pl.pallas_call(place_kernel, out_shape=(jax.ShapeDtypeStruct((16, ROWS, w...  2.05 us

profile of v5, /device:TPU:1, one launch (start us, length us, event | category | flops | bytes accessed | tf_op | source)
XLA Modules:
  0.0 60.4 jit_solution(1259268286276179952)
XLA Ops:
  0.6 57.8 %shard_map.103 = (bf16[48,32,1024]{2,1,0:T(8,128)(2,1)S(1)}, bf16[16,16,16,128]{3,2,1,0:T(8,128)(2,1)S(1)}, f32[8,128]{1,0:T(8,128)S(1)}) custom-call(bf16[8,256,256]{2,1,0:T(8,128)(2,1)} %bitcast.3, s32[384]{0:T(512)} %owner_in.1, s32[4,384]{1,0:T(4,128)} %bitcast.4, s32[384]{0:T(512)} %pattern_index_in.1, f32[4,64]{1,0:T(4,128)} %bitcast.5, ...), custom_call_target="tpu_custom_call" | custom-call | tf_op jit(solution)/shard_map/pallas_call | solution.py:445
  58.4 2.0 %shard_map.104 = (bf16[16,32,1024]{2,1,0:T(8,128)(2,1)}, bf16[48,32,1024]{2,1,0:T(8,128)(2,1)}, f32[48]{0:T(128)}) custom-call(bf16[48,32,1024]{2,1,0:T(8,128)(2,1)S(1)} %get-tuple-element.6.done, bf16[16,16,16,128]{3,2,1,0:T(8,128)(2,1)S(1)} %get-tuple-element.7.last, f32[8,128]{1,0:T(8,128)S(1)} %get-tuple-element.8.score), custom_call_target="tpu_custom_call" | custom-call | tf_op jit(solution)/shard_map/pallas_call | solution.py:492

commit v6 on v5

--- a/solution.py
+++ b/solution.py
@@ -159,19 +159,22 @@
 
     pl.semaphore_wait(barrier, len(ORDER) + N_PIX - 1)
 
-    inner, outer = pl.ds(2, GROUPS), pl.ds(0, 2)
+    inner = pl.ds(2, GROUPS)
+    top, bottom, head, foot = 0, 1, 2, GROUPS + 1
     halo = [
+        (pack_right.at[inner], left.at[inner], (0, 1)),
+        (pack_left.at[inner], right.at[inner], (0, -1)),
         (xs.at[GROUPS], xs.at[0], (1, 0)),
         (xs.at[1], xs.at[GROUPS + 1], (-1, 0)),
-        (pack_right.at[inner], left.at[inner], (0, 1)),
-        (pack_left.at[inner], right.at[inner], (0, -1)),
-        (pack_right.at[outer], left.at[outer], (0, 1)),
-        (pack_left.at[outer], right.at[outer], (0, -1)),
+        (left.at[foot], left.at[top], (1, 0)),
+        (right.at[foot], right.at[top], (1, 0)),
+        (left.at[head], left.at[bottom], (-1, 0)),
+        (right.at[head], right.at[bottom], (-1, 0)),
     ]
     halo = [
         remote(src, dst, halo_send.at[i], halo_recv.at[i], device(*to)) for i, (src, dst, to) in enumerate(halo)
     ]
-    for copy in halo[:4]:
+    for copy in halo[:2]:
         copy.start()
 
     def all_of(ref, sem, count):
@@ -189,12 +192,15 @@
         for i, (dz, dy) in (order[::-1] if TURNED[q] else order)[begin:end]:
             to = peer(dz, dy)
             copies.append(remote(out.at[q, to], target.at[mz], part_send.at[q], part_recv.at[q], {"mz": to}))
-        if begin == 0:
+        if begin < end == 15:
             copies.append(pltpu.make_async_copy(out.at[q, mz], target.at[mz], part_own.at[q]))
         for copy in copies:
             copy.start()
 
-    send(0, raw, 0, 8)
+    send(0, raw, 0, 2)
+    for copy in halo[2:4]:
+        copy.start()
+    send(0, raw, 2, 5)
 
     loads[2].wait()
     blur_high, blur_low, blur_sides = blur[:, 0:256], blur[:, 256:512], blur[:, 512:576]
@@ -228,6 +234,11 @@
 
     for copy in halo[:2]:
         copy.wait()
+    for copy in halo[4:]:
+        copy.start()
+    send(0, raw, 5, 15)
+    for copy in halo[2:4]:
+        copy.wait()
 
     @pl.when(pix == 0)
     def _():
@@ -237,15 +248,21 @@
     def _():
         xs[GROUPS + 1] = jnp.zeros(xs.shape[1:], BF16)
 
-    pack(0)
-    pack(GROUPS + 1)
+    for g in (0, GROUPS + 1):
+        columns_own(g)
+        pack_left[slot_of(g)] = dot(pick[0:16], xs[g]).astype(BF16)
     for copy in halo[4:]:
-        copy.start()
-    send(0, raw, 8, 15)
-    columns_own(0)
-    columns_own(GROUPS + 1)
-    for copy in halo[2:]:
-        copy.wait()
+        copy.wait()
+
+    @pl.when(pix == 0)
+    def _():
+        left[top] = jnp.zeros(left.shape[1:], BF16)
+        right[top] = jnp.zeros(right.shape[1:], BF16)
+
+    @pl.when(pix == N_PIX - 1)
+    def _():
+        left[bottom] = jnp.zeros(left.shape[1:], BF16)
+        right[bottom] = jnp.zeros(right.shape[1:], BF16)
 
     @pl.when(mz == 0)
     def _():
@@ -289,7 +306,7 @@
             out[q, d] = rolled_tiles([tile[d * 16 : (d + 1) * 16] for tile in tiles])
 
     product(1)
-    send(1, land.at[0], 0, 8)
+    send(1, land.at[0], 0, 11)
     product(2)
     product(3)
 
@@ -341,7 +358,7 @@
         small.append(remote(note.at[to], notes.at[mz], note_send, note_recv, {"mz": to}))
     for copy in small:
         copy.start()
-    send(1, land.at[0], 8, 15)
+    send(1, land.at[0], 11, 15)
     send(2, land.at[1], 0, 15)
 
     wait_part(0, raw)
@@ -472,8 +489,8 @@
             pltpu.VMEM((1, 128), F32),
             pltpu.VMEM((N_PIX, 1, 128), F32),
             dma((len(inputs),)),
-            dma((6,)),
-            dma((6,)),
+            dma((8,)),
+            dma((8,)),
             dma((PARTS,)),
             dma((PARTS,)),
             dma((PARTS,)),

time: 60.7 us -> 60.4 us (level)
  no operation moved by 1% of the time
where the time goes in v6:
time: 60.4 us; the launch traced here: 60.2 us
  Pallas kernels  59.6 us (99%)
  between operations  0.64 us (1%)
    pallas_call x1, Pallas kernels, body(): pl.pallas_call(produce_kernel, out_shape=(jax.ShapeDtypeStruct((48, ROWS,...  57.6 us
    pallas_call x1, Pallas kernels, body(): pl.pallas_call(place_kernel, out_shape=(jax.ShapeDtypeStruct((16, ROWS, w...  2.05 us

profile of v6, /device:TPU:1, one launch (start us, length us, event | category | flops | bytes accessed | tf_op | source)
XLA Modules:
  0.0 60.2 jit_solution(2192896471700088845)
XLA Ops:
  0.6 57.6 %shard_map.103 = (bf16[48,32,1024]{2,1,0:T(8,128)(2,1)S(1)}, bf16[16,16,16,128]{3,2,1,0:T(8,128)(2,1)S(1)}, f32[8,128]{1,0:T(8,128)S(1)}) custom-call(bf16[8,256,256]{2,1,0:T(8,128)(2,1)} %bitcast.3, s32[384]{0:T(512)} %owner_in.1, s32[4,384]{1,0:T(4,128)} %bitcast.4, s32[384]{0:T(512)} %pattern_index_in.1, f32[4,64]{1,0:T(4,128)} %bitcast.5, ...), custom_call_target="tpu_custom_call" | custom-call | tf_op jit(solution)/shard_map/pallas_call | solution.py:462
  58.2 2.0 %shard_map.104 = (bf16[16,32,1024]{2,1,0:T(8,128)(2,1)}, bf16[48,32,1024]{2,1,0:T(8,128)(2,1)}, f32[48]{0:T(128)}) custom-call(bf16[48,32,1024]{2,1,0:T(8,128)(2,1)S(1)} %get-tuple-element.6.done, bf16[16,16,16,128]{3,2,1,0:T(8,128)(2,1)S(1)} %get-tuple-element.7.last, f32[8,128]{1,0:T(8,128)S(1)} %get-tuple-element.8.score), custom_call_target="tpu_custom_call" | custom-call | tf_op jit(solution)/shard_map/pallas_call | solution.py:509

commit v7 on v6

--- a/solution.py
+++ b/solution.py
@@ -104,7 +104,7 @@
 def produce_kernel(
     spectra, owner_in, peaks_in, pattern_index_in, patterns_in, blur_in, more_in, wide_in, done, last, score,
     owner, peaks, pattern_index, patterns, blur, more, wide, xs, pack_left, pack_right, left, right, ys, ion, coef,
-    form, out, raw, land, rows_wide, joined, note, notes, total, totals,
+    form, out, raw, land, rows_wide, joined, note, notes, total, totals, score_here,
     load_sem, halo_send, halo_recv, part_send, part_recv, part_own, rows_send, rows_recv, done_sem,
     note_send, note_recv, total_send, total_recv,
 ):
@@ -128,7 +128,7 @@
     sources = [spectra, more_in, blur_in, owner_in, peaks_in, pattern_index_in, patterns_in, wide_in]
     targets = [xs.at[pl.ds(1, GROUPS)], more, blur, owner, peaks, pattern_index, patterns, wide]
     loads = [pltpu.make_async_copy(src, dst, load_sem.at[i]) for i, (src, dst) in enumerate(zip(sources, targets))]
-    for copy in loads:
+    for copy in loads[:2]:
         copy.start()
 
     barrier = pltpu.get_barrier_semaphore()
@@ -136,6 +136,9 @@
         pl.semaphore_signal(barrier, inc=1, device_id={"mz": peer(dz, dy)}, device_id_type=MESH)
     for dp in (1, 7, 2, 3, 4, 5, 6):
         pl.semaphore_signal(barrier, inc=1, device_id=device(dp, 0), device_id_type=MESH)
+
+    for copy in loads[2:]:
+        copy.start()
 
     for copy in loads[:2]:
         copy.wait()
@@ -420,14 +423,16 @@
     totals[pix] = total[...]
     final = jnp.sum(totals[...], axis=0)
     final = final / (pltpu.roll(final, 64, 1) + 1e-5)
-    score[...] = jnp.broadcast_to(final, (8, 128))
+    score_here[...] = jnp.broadcast_to(final, (8, 128))
+    stores.append(pltpu.make_async_copy(score_here, score, done_sem.at[3]))
+    stores[-1].start()
 
     for q in (1, 2):
         wait_part(q, land.at[q - 1])
         at = pl.ds(q * 16, 16)
         join_strips(land.at[q - 1], joined.at[at])
         stores.append(pltpu.make_async_copy(joined.at[at], done.at[at], done_sem.at[q]))
-        stores[q].start()
+        stores[-1].start()
     for copy in stores:
         copy.wait()
     wait_part(3, last)
@@ -467,7 +472,7 @@
             jax.ShapeDtypeStruct((8, 128), F32),
         ),
         in_specs=[hbm] * len(inputs),
-        out_specs=(free, free, vmem),
+        out_specs=(free, free, free),
         scratch_shapes=[pltpu.VMEM(x.shape, x.dtype) for x in inputs[1:]]
         + [
             pltpu.VMEM((GROUPS + 2, 256, BINS), BF16),
@@ -488,6 +493,7 @@
             pltpu.VMEM((N_MZ, 1, 128), F32),
             pltpu.VMEM((1, 128), F32),
             pltpu.VMEM((N_PIX, 1, 128), F32),
+            pltpu.VMEM((8, 128), F32),
             dma((len(inputs),)),
             dma((8,)),
             dma((8,)),
@@ -496,7 +502,7 @@
             dma((PARTS,)),
             dma((2,)),
             dma((2,)),
-            dma((3,)),
+            dma((4,)),
             dma,
             dma,
             dma,

time: 60.4 us -> 60.4 us (level)
  no operation moved by 1% of the time
where the time goes in v7:
time: 60.4 us; the launch traced here: 60.2 us
  Pallas kernels  59.6 us (99%)
  between operations  0.64 us (1%)
    pallas_call x1, Pallas kernels, body(): pl.pallas_call(produce_kernel, out_shape=(jax.ShapeDtypeStruct((48, ROWS,...  57.6 us
    pallas_call x1, Pallas kernels, body(): pl.pallas_call(place_kernel, out_shape=(jax.ShapeDtypeStruct((16, ROWS, w...  2.05 us

profile of v7, /device:TPU:1, one launch (start us, length us, event | category | flops | bytes accessed | tf_op | source)
XLA Modules:
  0.0 60.2 jit_solution(14386011902998625286)
XLA Ops:
  0.6 57.6 %shard_map.103 = (bf16[48,32,1024]{2,1,0:T(8,128)(2,1)S(1)}, bf16[16,16,16,128]{3,2,1,0:T(8,128)(2,1)S(1)}, f32[8,128]{1,0:T(8,128)S(1)}) custom-call(bf16[8,256,256]{2,1,0:T(8,128)(2,1)} %bitcast.3, s32[384]{0:T(512)} %owner_in.1, s32[4,384]{1,0:T(4,128)} %bitcast.4, s32[384]{0:T(512)} %pattern_index_in.1, f32[4,64]{1,0:T(4,128)} %bitcast.5, ...), custom_call_target="tpu_custom_call" | custom-call | tf_op jit(solution)/shard_map/pallas_call | solution.py:467
  58.2 2.0 %shard_map.104 = (bf16[16,32,1024]{2,1,0:T(8,128)(2,1)}, bf16[48,32,1024]{2,1,0:T(8,128)(2,1)}, f32[48]{0:T(128)}) custom-call(bf16[48,32,1024]{2,1,0:T(8,128)(2,1)S(1)} %get-tuple-element.6.done, bf16[16,16,16,128]{3,2,1,0:T(8,128)(2,1)S(1)} %get-tuple-element.7.last, f32[8,128]{1,0:T(8,128)S(1)} %get-tuple-element.8.score), custom_call_target="tpu_custom_call" | custom-call | tf_op jit(solution)/shard_map/pallas_call | solution.py:515
